TPU v7x, 512 devices: a whole 4x8x8 slice. The times are simulated.
512 devices in a mesh: pt: 64 (over x, y, core), case: 8 (over z).
Axes of the slice: x: 4, y: 8, z: 8, core: 2. Of those that a mesh axis runs over, the one named last changes fastest.
Arguments:
- points: bfloat16 [8, 32768, 256], P('case', 'pt')
- cotangent: bfloat16 [8, 32768, 256], P('case', 'pt'), may hold values from -6 to 6
- to_hilbert: int32 [8, 32768], P('case', 'pt'), may hold values from 0 to 32767, as said below
- from_hilbert: int32 [8, 32768], P('case', 'pt'), may hold values from 0 to 32767, as said below
- ln_gain: float32 [256], replicated, may hold values from 0.1 to 1.9
- ln_bias: float32 [256], replicated, may hold values from -3 to 3
- w_qkv: bfloat16 [256, 768], replicated, may hold values from -0.5 to 0.5
- b_qkv: float32 [768], replicated, may hold values from -3 to 3
- w_out: bfloat16 [256, 256], replicated, may hold values from -0.375 to 0.375
- b_out: float32 [256], replicated, may hold values from -3 to 3
Outputs:
- output: bfloat16 [8, 32768, 256], P('case', 'pt')
- grad_points: bfloat16 [8, 32768, 256], P('case', 'pt')
- grad_w_qkv: float32 [256, 768], replicated
- grad_b_qkv: float32 [768], replicated
- grad_w_out: float32 [256, 256], replicated
- grad_b_out: float32 [256], replicated
- grad_gain: float32 [256], replicated
- grad_bias: float32 [256], replicated
Inputs may be any that keep to these rules, and one draw needn't show every extreme that they name: `to_hilbert`: for each slab a permutation. Shard s holds Z positions and Hilbert positions s * 512 to (s + 1) * 512 - 1; every point's Hilbert position lies in its own shard or a neighbouring one, and a point that changes shard lies in the half of its shard nearer to that neighbour in both orders. Across each boundary as many points cross in one direction as in the other, at most 256, and exactly 256 at some boundary of every slab. `from_hilbert`: the inverse permutation of to_hilbert for each slab.
All inputs are finite; a program needn't handle non-finite values.
Results may differ from a plain program's by a relative error of at most 0.005.
The roundings to bfloat16 on the way count: a program that leaves them out, or rounds other values in their place, can miss the bound.
Values may be sent and summed in bfloat16 or wider, within the bound.
A program may use at most 64 MiB of HBM per device.

v0:
```python
import math

import jax
import jax.numpy as jnp
from jax import lax
from jax.sharding import PartitionSpec as P

D = 256
HEADS = 8
HEAD = 32
PATCH = 256


epsilon = 1e-05


def extended(cells, sides, width):
    for axis, dim in sides:
        count = lax.axis_size(axis)
        ends = count - 1
        head = lax.slice_in_dim(cells, 0, width, axis=dim)
        tail = lax.slice_in_dim(cells, cells.shape[dim] - width, cells.shape[dim], axis=dim)
        cells = jnp.concatenate(
            [
                lax.ppermute(tail, axis, [(i, (i + 1) % count) for i in range(ends)]),
                cells,
                lax.ppermute(head, axis, [((i + 1) % count, i) for i in range(ends)]),
            ],
            axis=dim,
        )
    return cells


def plan_routes(target_local, source_local, length, capacity):
    go_left = target_local < 0
    go_right = target_local >= length
    rank_left = jnp.cumsum(go_left.astype(jnp.int32)) - 1
    rank_right = jnp.cumsum(go_right.astype(jnp.int32)) - 1
    slot_left = jnp.where(go_left, rank_left, capacity)
    slot_right = jnp.where(go_right, rank_right, capacity)
    zorder_index = jnp.where(
        go_left,
        length + rank_left,
        jnp.where(go_right, length + capacity + rank_right, target_local),
    )
    from_left = source_local < 0
    from_right = source_local >= length
    mark_left = (
        jnp.zeros((length,), jnp.int32)
        .at[jnp.where(from_left, source_local + length, length)]
        .set(1, mode="drop")
    )
    mark_right = (
        jnp.zeros((length,), jnp.int32)
        .at[jnp.where(from_right, source_local - length, length)]
        .set(1, mode="drop")
    )
    arrival_left = jnp.take(
        jnp.cumsum(mark_left) - 1, jnp.clip(source_local + length, 0, length - 1)
    )
    arrival_right = jnp.take(
        jnp.cumsum(mark_right) - 1, jnp.clip(source_local - length, 0, length - 1)
    )
    hilbert_index = jnp.where(
        from_left,
        length + arrival_left,
        jnp.where(from_right, length + capacity + arrival_right, source_local),
    )
    back_left = jnp.where(from_left, arrival_left, capacity)
    back_right = jnp.where(from_right, arrival_right, capacity)
    return (slot_left, slot_right, hilbert_index, back_left, back_right, zorder_index)


def depart(payload, slot_left, slot_right, capacity):
    empty = jnp.zeros((capacity, payload.shape[1]), payload.dtype)
    to_left = empty.at[slot_left].set(payload, mode="drop")
    to_right = empty.at[slot_right].set(payload, mode="drop")
    return jnp.concatenate([to_left, to_right], axis=0)


def settle(arrived, own_rows, index_rows, capacity):
    stacked = jnp.concatenate([own_rows, arrived[:capacity], arrived[3 * capacity :]], axis=0)
    return jnp.take(stacked, index_rows, axis=0)


def attention_weights(query_rows, key_rows, softmax_scale):
    scores = (
        jnp.einsum("nqhd,nkhd->nhqk", query_rows, key_rows, preferred_element_type=jnp.float32)
        * softmax_scale
    )
    exponent = jnp.exp(scores)
    return exponent / jnp.sum(exponent, axis=-1, keepdims=True)


def forward_pass(hilbert_points, params):
    ln_gain, ln_bias, w_qkv, b_qkv, w_out, b_out = params
    length = hilbert_points.shape[0]
    patches = length // PATCH
    features = hilbert_points.astype(jnp.float32)
    centered = features - jnp.mean(features, axis=-1, keepdims=True)
    inverse_std = lax.rsqrt(jnp.mean(centered * centered, axis=-1, keepdims=True) + epsilon)
    standard = centered * inverse_std
    normed = (standard * ln_gain + ln_bias).astype(jnp.bfloat16)
    projected = (jnp.dot(normed, w_qkv, preferred_element_type=jnp.float32) + b_qkv).astype(
        jnp.bfloat16
    )
    triple = projected.reshape(patches, PATCH, 3, HEADS, HEAD)
    softmax_scale = 1.0 / math.sqrt(HEAD)
    pieces = []
    for head_start in range(HEADS):
        query_rows = triple[:, :, 0, head_start : head_start + 1]
        key_rows = triple[:, :, 1, head_start : head_start + 1]
        value_rows = triple[:, :, 2, head_start : head_start + 1]
        probability = attention_weights(query_rows, key_rows, softmax_scale)
        pieces.append(
            jnp.einsum(
                "nhqk,nkhd->nqhd",
                probability.astype(jnp.bfloat16),
                value_rows,
                preferred_element_type=jnp.float32,
            ).astype(jnp.bfloat16)
        )
    attended = jnp.concatenate(pieces, axis=2).reshape(length, D)
    branch = jnp.dot(attended, w_out, preferred_element_type=jnp.float32) + b_out
    result = (features + branch).astype(jnp.bfloat16)
    return (result, standard, inverse_std, normed, triple, attended)


def backward_pass(hilbert_cotangent, saved_state, params):
    ln_gain, ln_bias, w_qkv, b_qkv, w_out, b_out = params
    result, standard, inverse_std, normed, triple, attended = saved_state
    length = hilbert_cotangent.shape[0]
    patches = length // PATCH
    softmax_scale = 1.0 / math.sqrt(HEAD)
    d_attended = jnp.dot(hilbert_cotangent, w_out.T, preferred_element_type=jnp.float32).astype(
        jnp.bfloat16
    )
    d_heads = d_attended.reshape(patches, PATCH, HEADS, HEAD)
    pieces = []
    for head_start in range(HEADS):
        query_rows = triple[:, :, 0, head_start : head_start + 1]
        key_rows = triple[:, :, 1, head_start : head_start + 1]
        value_rows = triple[:, :, 2, head_start : head_start + 1]
        d_group = d_heads[:, :, head_start : head_start + 1]
        probability = attention_weights(query_rows, key_rows, softmax_scale)
        weights_low = probability.astype(jnp.bfloat16)
        d_values = jnp.einsum(
            "nhqk,nqhd->nkhd", weights_low, d_group, preferred_element_type=jnp.float32
        )
        d_prob = jnp.einsum(
            "nqhd,nkhd->nhqk", d_group, value_rows, preferred_element_type=jnp.float32
        )
        d_scores = (
            probability
            * (d_prob - jnp.sum(probability * d_prob, axis=-1, keepdims=True))
            * softmax_scale
        ).astype(jnp.bfloat16)
        d_query = jnp.einsum(
            "nhqk,nkhd->nqhd", d_scores, key_rows, preferred_element_type=jnp.float32
        )
        d_keys = jnp.einsum(
            "nhqk,nqhd->nkhd", d_scores, query_rows, preferred_element_type=jnp.float32
        )
        pieces.append(jnp.stack([d_query, d_keys, d_values], axis=2))
    d_projected = jnp.concatenate(pieces, axis=3).reshape(length, 3 * D).astype(jnp.bfloat16)
    d_normed = jnp.dot(d_projected, w_qkv.T, preferred_element_type=jnp.float32)
    scaled_grad = d_normed * ln_gain
    d_input = inverse_std * (
        scaled_grad
        - jnp.mean(scaled_grad, axis=-1, keepdims=True)
        - standard * jnp.mean(scaled_grad * standard, axis=-1, keepdims=True)
    )
    grad_rows = (hilbert_cotangent.astype(jnp.float32) + d_input).astype(jnp.bfloat16)
    weight_terms = (
        jnp.einsum("pi,pj->ij", normed, d_projected, preferred_element_type=jnp.float32),
        jnp.sum(d_projected.astype(jnp.float32), axis=0),
        jnp.einsum("pi,pj->ij", attended, hilbert_cotangent, preferred_element_type=jnp.float32),
        jnp.sum(hilbert_cotangent.astype(jnp.float32), axis=0),
        jnp.sum(d_normed * standard, axis=0),
        jnp.sum(d_normed, axis=0),
    )
    return (grad_rows, weight_terms)


def on_device(
    points, cotangent, to_hilbert, from_hilbert, ln_gain, ln_bias, w_qkv, b_qkv, w_out, b_out
):
    own_points = points[0]
    own_cotangent = cotangent[0]
    length = own_points.shape[0]
    capacity = length // 2
    offset = lax.axis_index("pt") * length
    slot_left, slot_right, hilbert_index, back_left, back_right, zorder_index = plan_routes(
        to_hilbert[0] - offset, from_hilbert[0] - offset, length, capacity
    )
    params = (ln_gain, ln_bias, w_qkv, b_qkv, w_out, b_out)
    arrived_points = extended(
        depart(own_points, slot_left, slot_right, capacity), (("pt", 0),), capacity
    )
    saved_state = forward_pass(settle(arrived_points, own_points, hilbert_index, capacity), params)
    returned_output = extended(
        depart(saved_state[0], back_left, back_right, capacity), (("pt", 0),), capacity
    )
    output = settle(returned_output, saved_state[0], zorder_index, capacity)
    arrived_cotangent = extended(
        depart(own_cotangent, slot_left, slot_right, capacity), (("pt", 0),), capacity
    )
    grad_rows, weight_terms = backward_pass(
        settle(arrived_cotangent, own_cotangent, hilbert_index, capacity), saved_state, params
    )
    returned_grad = extended(
        depart(grad_rows, back_left, back_right, capacity), (("pt", 0),), capacity
    )
    grad_points = settle(returned_grad, grad_rows, zorder_index, capacity)
    sums = lax.psum(
        (
            weight_terms[0],
            weight_terms[1],
            weight_terms[2],
            weight_terms[3],
            weight_terms[4],
            weight_terms[5],
        ),
        ("pt", "case"),
    )
    total_points = lax.axis_size("pt") * lax.axis_size("case") * length
    factor = 1.0 / math.sqrt(total_points)
    return (
        output[None],
        grad_points[None],
        sums[0] * factor,
        sums[1] * factor,
        sums[2] * factor,
        sums[3] * factor,
        sums[4] * factor,
        sums[5] * factor,
    )


def solution(mesh):
    in_specs = (
        P("case", "pt", None),
        P("case", "pt", None),
        P("case", "pt"),
        P("case", "pt"),
        P(),
        P(),
        P(),
        P(),
        P(),
        P(),
    )
    out_specs = (P("case", "pt", None), P("case", "pt", None), P(), P(), P(), P(), P(), P())
    return jax.shard_map(
        on_device, mesh=mesh, in_specs=in_specs, out_specs=out_specs, check_vma=False
    )
```

profile of v0, /device:TPU:23, one launch (start us, length us, event | category | flops | bytes accessed | tf_op | source)
XLA Modules:
  0.0 530.2 jit_solution(10503999546369005947)
XLA Ops:
  9.3 2.7 scatter_custom_fusion
  12.0 3.8 collective-permute-start
  15.8 2.7 scatter_custom_fusion.6
  18.5 1.9 collective-permute-start.4
  20.4 2.3 scatter_custom_fusion.1
  22.8 2.4 collective-permute-start.1
  25.2 2.3 scatter_custom_fusion.7
  27.5 2.0 collective-permute-start.5
  29.6 2.4 scatter_custom_fusion.3
  32.7 2.7 scatter_custom_fusion.2
  36.0 3.5 gather_fusion.1
  40.1 3.5 gather_fusion
  45.5 2.0 gather_fusion.2
  49.1 1.2 fusion.248
  51.2 2.0 gather_fusion.4
  69.8 1.6 convolution_bitcast_fusion.11
  71.4 1.6 convolution_bitcast_fusion.10
  73.1 1.1 fusion.121
  74.2 1.6 convolution_bitcast_fusion.12
  75.7 1.8 fusion.179
  77.6 2.1 convolution_bitcast_fusion.14
  79.6 2.1 convolution_bitcast_fusion.13
  81.7 1.9 fusion.123
  83.6 1.9 convolution_bitcast_fusion.15
  85.5 1.8 fusion.178
  87.3 2.4 convolution_bitcast_fusion.17
  89.7 2.4 convolution_bitcast_fusion.16
  92.1 1.9 fusion.125
  94.0 1.9 convolution_bitcast_fusion.18
  95.9 1.8 fusion.177
  97.7 2.4 convolution_bitcast_fusion.20
  100.1 2.4 convolution_bitcast_fusion.19
  107.8 1.9 fusion.109
  109.8 1.6 fusion.244
  114.9 10.5 %scatter_custom_fusion.5 = bf16[256,256]{1,0:T(8,128)(2,1)S(1)} fusion(s32[512]{0:T(512)} %compare_select_fusion.11, bf16[512,256]{1,0:T(8,128)(2,1)S(1)} %fusion.49, bf16[]{:T(256)} %constant.27.clone.1), kind=kCustom, calls=%fused_computation.243 | custom fusion | bytes 131584 | tf_op jit(solution)/shard_map/scatter | solution.py:76
  125.5 2.5 scatter_custom_fusion.4
  128.5 2.5 scatter_custom_fusion.9
  130.9 2.5 scatter_custom_fusion.8
  133.4 4.2 collective-permute-start.2
  137.6 1.9 collective-permute-start.3
  139.7 103.3 %all-reduce = (f32[768]{0:T(1024)S(1)}, f32[256]{0:T(256)S(1)}, f32[256]{0:T(256)S(1)}, f32[256]{0:T(256)S(1)}) all-reduce(f32[768]{0:T(1024)S(1)} %reduce_sum.271, f32[256]{0:T(256)S(1)} %copy-done.46, f32[256]{0:T(256)S(1)} %copy-done.44, f32[256]{0:T(256)S(1)} %copy-done.45), channel_id=1, replica_groups=mesh['pt'=64,'case'=8] {'pt','case'}, use_global_device_ids=true, to_apply=%region_40.43 | all-reduce | flops 1536 | bytes 12288 | tf_op jit(solution)/shard_map/psum | solution.py:215
  243.5 2.8 collective-permute-start.6
  246.3 1.9 collective-permute-start.7
  249.4 2.0 gather_fusion.3
  251.4 1.2 collective-permute-done.7
  252.6 2.0 gather_fusion.5
  255.5 264.8 %all-reduce.4.cloned.1.call-done = (f32[256,768]{1,0:T(8,128)}, f32[256,256]{1,0:T(8,128)}) async-done(((f32[256,768]{1,0:T(8,128)}, f32[256,256]{1,0:T(8,128)}), (f32[256,768]{1,0:T(8,128)}, f32[256,256]{1,0:T(8,128)})) %all-reduce.4.cloned.1.call-update) | async-done | bytes 1048592 | tf_op jit(solution)/shard_map/psum | solution.py:215
  520.3 2.1 broadcast_multiply_fusion
  (226 shorter events, 37.2 us)
Async XLA Ops:
  7.2 40.8 %copy-start = (bf16[256,768]{1,0:T(8,128)(2,1)S(1)}, bf16[256,768]{1,0:T(8,128)(2,1)}, u32[]{:S(2)}) copy-start(bf16[256,768]{1,0:T(8,128)(2,1)} %param.20) | copy-start | bytes 1179652
  7.2 13.3 %copy-start.1 = (bf16[1,512,256]{2,1,0:T(8,128)(2,1)S(1)}, bf16[1,512,256]{2,1,0:T(8,128)(2,1)}, u32[]{:S(2)}) copy-start(bf16[1,512,256]{2,1,0:T(8,128)(2,1)} %param.14) | copy-start | bytes 786436
  7.2 18.0 %copy-start.2 = (bf16[1,512,256]{2,1,0:T(8,128)(2,1)S(1)}, bf16[1,512,256]{2,1,0:T(8,128)(2,1)}, u32[]{:S(2)}) copy-start(bf16[1,512,256]{2,1,0:T(8,128)(2,1)} %param.15) | copy-start | bytes 786436
  7.2 513.1 %all-reduce.4.cloned.1.call-start = ((), (), s32[]{:S(2)}) async-start(), calls=%async_computation | async-start | bytes 2097152 | tf_op jit(solution)/shard_map/psum | solution.py:215
  9.3 20.3 %copy-start.41 = (s32[1,512]{1,0:T(1,128)S(1)}, s32[1,512]{1,0:T(1,128)}, u32[]{:S(2)}) copy-start(s32[1,512]{1,0:T(1,128)} %param.17) | copy-start | bytes 6148
  12.0 33.4 %collective-permute-start = (bf16[256,256]{1,0:T(8,128)(2,1)S(1)}, bf16[256,256]{1,0:T(8,128)(2,1)S(1)}, u32[]{:S(2)}, u32[]{:S(2)}) collective-permute-start(bf16[256,256]{1,0:T(8,128)(2,1)S(1)} %scatter_custom_fusion), channel_id=1, source_target_pairs={{0,8},{8,16},{16,24},{24,32},{32,40},{40,48},{48,56},{56,64},{64,7... | collective-permute-start | bytes 393224 | tf_op jit(solution)/shard_map/ppermute | solution.py:25
  18.5 32.6 %collective-permute-start.4 = (bf16[256,256]{1,0:T(8,128)(2,1)S(1)}, bf16[256,256]{1,0:T(8,128)(2,1)S(1)}, u32[]{:S(2)}, u32[]{:S(2)}) collective-permute-start(bf16[256,256]{1,0:T(8,128)(2,1)S(1)} %scatter_custom_fusion.6), channel_id=1, source_target_pairs={{0,8},{8,16},{16,24},{24,32},{32,40},{40,48},{48,56},{56,64},{64,7... | collective-permute-start | bytes 393224 | tf_op jit(solution)/shard_map/ppermute | solution.py:25
  22.8 22.6 %collective-permute-start.1 = (bf16[256,256]{1,0:T(8,128)(2,1)S(1)}, bf16[256,256]{1,0:T(8,128)(2,1)S(1)}, u32[]{:S(2)}, u32[]{:S(2)}) collective-permute-start(bf16[256,256]{1,0:T(8,128)(2,1)S(1)} %scatter_custom_fusion.1), channel_id=1, source_target_pairs={{8,0},{16,8},{24,16},{32,24},{40,32},{48,40},{56,48},{64,56},{72,6... | collective-permute-start | bytes 393224 | tf_op jit(solution)/shard_map/ppermute | solution.py:27
  27.5 23.6 %collective-permute-start.5 = (bf16[256,256]{1,0:T(8,128)(2,1)S(1)}, bf16[256,256]{1,0:T(8,128)(2,1)S(1)}, u32[]{:S(2)}, u32[]{:S(2)}) collective-permute-start(bf16[256,256]{1,0:T(8,128)(2,1)S(1)} %scatter_custom_fusion.7), channel_id=1, source_target_pairs={{8,0},{16,8},{24,16},{32,24},{40,32},{48,40},{56,48},{64,56},{72,6... | collective-permute-start | bytes 393224 | tf_op jit(solution)/shard_map/ppermute | solution.py:27
  43.6 9.6 %copy-start.34 = (pred[512]{0:T(512)(128)(4,1)}, pred[512]{0:T(512)(128)(4,1)S(1)}, u32[]{:S(2)}) copy-start(pred[512]{0:T(512)(128)(4,1)S(1)} %get-tuple-element.23) | copy-start | bytes 1540
  45.5 2.6 copy-start.47
  45.5 2.6 copy-start.52
  45.5 2.6 copy-start.53
  50.3 5.2 copy-start.7
  50.3 12.2 %copy-start.9 = (bf16[2,256,1,1,32]{1,0,4,3,2:T(2,128)(2,1)}, bf16[2,256,1,1,32]{1,0,4,3,2:T(2,128)(2,1)S(1)}, u32[]{:S(2)}) copy-start(bf16[2,256,1,1,32]{1,0,4,3,2:T(2,128)(2,1)S(1)} %get-tuple-element.33) | copy-start | bytes 98308
  50.3 15.3 %copy-start.11 = (bf16[2,256,1,1,32]{1,0,4,3,2:T(2,128)(2,1)}, bf16[2,256,1,1,32]{1,0,4,3,2:T(2,128)(2,1)S(1)}, u32[]{:S(2)}) copy-start(bf16[2,256,1,1,32]{1,0,4,3,2:T(2,128)(2,1)S(1)} %get-tuple-element.36) | copy-start | bytes 98308
  50.4 17.3 %copy-start.23 = (bf16[2,256,1,1,32]{1,0,4,3,2:T(2,128)(2,1)}, bf16[2,256,1,1,32]{1,0,4,3,2:T(2,128)(2,1)S(1)}, u32[]{:S(2)}) copy-start(bf16[2,256,1,1,32]{1,0,4,3,2:T(2,128)(2,1)S(1)} %get-tuple-element.38) | copy-start | bytes 98308
  50.4 17.3 %copy-start.24 = (bf16[2,256,1,1,32]{1,0,4,3,2:T(2,128)(2,1)}, bf16[2,256,1,1,32]{1,0,4,3,2:T(2,128)(2,1)S(1)}, u32[]{:S(2)}) copy-start(bf16[2,256,1,1,32]{1,0,4,3,2:T(2,128)(2,1)S(1)} %get-tuple-element.37) | copy-start | bytes 98308
  51.1 2.0 copy-start.50
  54.4 13.6 %copy-start.17 = (bf16[2,256,1,32]{1,0,3,2:T(2,128)(2,1)}, bf16[2,256,1,32]{1,0,3,2:T(2,128)(2,1)S(1)}, u32[]{:S(2)}) copy-start(bf16[2,256,1,32]{1,0,3,2:T(2,128)(2,1)S(1)} %get-tuple-element.56) | copy-start | bytes 98308
  102.6 3.4 copy-start.22
  102.6 3.4 copy-start.31
  102.6 3.4 copy-start.32
  102.6 3.4 copy-start.21
  102.6 3.4 copy-start.29
  102.6 3.4 copy-start.30
  102.6 3.4 copy-start.20
  102.6 3.4 copy-start.27
  102.6 3.4 copy-start.28
  102.6 3.5 copy-start.19
  102.6 3.5 copy-start.25
  102.6 3.5 copy-start.26
  107.8 1.9 copy-start.54
  109.8 1.8 copy-start.3
  114.6 13.4 %copy-start.42 = (f32[512]{0:T(512)S(1)}, f32[512]{0:T(512)}, u32[]{:S(2)}) copy-start(f32[512]{0:T(512)} %get-tuple-element.11) | copy-start | bytes 6148
  114.6 13.4 %copy-start.43 = (f32[512]{0:T(512)S(1)}, f32[512]{0:T(512)}, u32[]{:S(2)}) copy-start(f32[512]{0:T(512)} %get-tuple-element.12) | copy-start | bytes 6148
  114.6 13.4 %copy-start.5 = (f32[512,256]{1,0:T(8,128)S(1)}, f32[512,256]{1,0:T(8,128)}, u32[]{:S(2)}) copy-start(f32[512,256]{1,0:T(8,128)} %get-tuple-element.67) | copy-start | bytes 1572868
  114.6 13.4 %copy-start.39 = (f32[512]{0:T(512)S(1)}, f32[512]{0:T(512)}, u32[]{:S(2)}) copy-start(f32[512]{0:T(512)} %copy-done.37) | copy-start | bytes 6148
  114.6 13.4 %copy-start.49 = (f32[256]{0:T(256)S(1)}, f32[256]{0:T(256)}, u32[]{:S(2)}) copy-start(f32[256]{0:T(256)} %param.18) | copy-start | bytes 3076
  128.0 11.6 %copy-start.44 = (f32[256]{0:T(256)S(1)}, f32[256]{0:T(256)}, u32[]{:S(2)}) copy-start(f32[256]{0:T(256)} %get-tuple-element.10) | copy-start | bytes 3076
  128.0 11.6 %copy-start.45 = (f32[256]{0:T(256)S(1)}, f32[256]{0:T(256)}, u32[]{:S(2)}) copy-start(f32[256]{0:T(256)} %get-tuple-element.13) | copy-start | bytes 3076
  128.0 11.6 %copy-start.46 = (f32[256]{0:T(256)S(1)}, f32[256]{0:T(256)}, u32[]{:S(2)}) copy-start(f32[256]{0:T(256)} %get-tuple-element.14) | copy-start | bytes 3076
  133.4 116.0 %collective-permute-start.2 = (bf16[256,256]{1,0:T(8,128)(2,1)S(1)}, bf16[256,256]{1,0:T(8,128)(2,1)S(1)}, u32[]{:S(2)}, u32[]{:S(2)}) collective-permute-start(bf16[256,256]{1,0:T(8,128)(2,1)S(1)} %scatter_custom_fusion.4), channel_id=1, source_target_pairs={{0,8},{8,16},{16,24},{24,32},{32,40},{40,48},{48,56},{56,64},{64,7... | collective-permute-start | bytes 393224 | tf_op jit(solution)/shard_map/ppermute | solution.py:25
  137.6 111.7 %collective-permute-start.3 = (bf16[256,256]{1,0:T(8,128)(2,1)S(1)}, bf16[256,256]{1,0:T(8,128)(2,1)S(1)}, u32[]{:S(2)}, u32[]{:S(2)}) collective-permute-start(bf16[256,256]{1,0:T(8,128)(2,1)S(1)} %scatter_custom_fusion.5), channel_id=1, source_target_pairs={{8,0},{16,8},{24,16},{32,24},{40,32},{48,40},{56,48},{64,56},{72,6... | collective-permute-start | bytes 393224 | tf_op jit(solution)/shard_map/ppermute | solution.py:27
  243.5 7.9 %collective-permute-start.6 = (bf16[256,256]{1,0:T(8,128)(2,1)S(1)}, bf16[256,256]{1,0:T(8,128)(2,1)S(1)}, u32[]{:S(2)}, u32[]{:S(2)}) collective-permute-start(bf16[256,256]{1,0:T(8,128)(2,1)S(1)} %scatter_custom_fusion.8), channel_id=1, source_target_pairs={{0,8},{8,16},{16,24},{24,32},{32,40},{40,48},{48,56},{56,64},{64,7... | collective-permute-start | bytes 393224 | tf_op jit(solution)/shard_map/ppermute | solution.py:25
  246.3 6.3 %collective-permute-start.7 = (bf16[256,256]{1,0:T(8,128)(2,1)S(1)}, bf16[256,256]{1,0:T(8,128)(2,1)S(1)}, u32[]{:S(2)}, u32[]{:S(2)}) collective-permute-start(bf16[256,256]{1,0:T(8,128)(2,1)S(1)} %scatter_custom_fusion.9), channel_id=1, source_target_pairs={{8,0},{16,8},{24,16},{32,24},{40,32},{48,40},{56,48},{64,56},{72,6... | collective-permute-start | bytes 393224 | tf_op jit(solution)/shard_map/ppermute | solution.py:27
  252.6 2.0 copy-start.40
  520.3 2.1 copy-start.18
  (17 other events, 17.8 us)
Sparse Core Ops, SparseCore 0:
  248.4 271.8 all-reduce.3
where the time goes:
time: 541 us; the launch traced here: 530 us
  waiting for transfers between devices  266 us (49%)
  blocking collectives  103 us (19%)
  local copies, waits for them, and re-layouts  54.9 us (10%)
  matrix products  54.7 us (10%)
  starting transfers between devices  20.9 us (4%)
  between operations  15.4 us (3%)
  other arithmetic  15 us (3%)
    psum x1, waiting for transfers between devices, on_device(): lax.psum((weight_terms[0], weight_terms[1], weight_terms[2], weight_terms...  265 us
    psum x1, blocking collectives, on_device(): lax.psum((weight_terms[0], weight_terms[1], weight_terms[2], weight_terms...  103 us
    scatter x4, local copies, waits for them, and re-layouts, depart(): to_left = empty.at[slot_left].set(payload, mode='drop')  17.7 us
    ppermute x4, starting transfers between devices, extended(): lax.ppermute(tail, axis, [(i, (i + 1) % count) for i in range(ends)])  12.7 us
    dot_general x8, matrix products, backward_pass(): jnp.einsum('nhqk,nqhd->nkhd', d_scores, query_rows, preferred_element_typ...  12 us
    dot_general x8, matrix products, backward_pass(): jnp.einsum('nhqk,nkhd->nqhd', d_scores, key_rows, preferred_element_type=...  11.9 us
  transfers between devices with their start and end apart: 9, of which 2 were waited for; matrix products, arithmetic and copies ran while one was open for 7% of the time, Pallas kernels for 0%

commit v1 on v0

v1 whole, which is shorter than its diff:
```python
import functools
import math

import jax
import jax.numpy as jnp
from jax import lax
from jax.experimental import pallas as pl
from jax.experimental.pallas import tpu as pltpu
from jax.sharding import PartitionSpec as P

D = 256
HEADS = 8
HEAD = 32
PATCH = 256
LEN = 512
HALF = 256
WIN = 1024
TILES = 32
epsilon = 1e-05
VMEM_LIMIT = 60 * 1024 * 1024
SCALE = 1.0 / math.sqrt(HEAD)
EXP2_SCALE = SCALE * math.log2(math.e)

MESH = pl.DeviceIdType.MESH
F32 = jnp.float32
BF16 = jnp.bfloat16


def nn(a, b):
    return lax.dot_general(a, b, (((1,), (0,)), ((), ())), preferred_element_type=F32)


def nt(a, b):
    return lax.dot_general(a, b, (((1,), (1,)), ((), ())), preferred_element_type=F32)


def one_hot(index_row, low, width):
    columns = [
        jnp.transpose(jnp.broadcast_to(index_row[:, a : a + 128], (128, 128))) for a in (0, 128)
    ]
    column = jnp.concatenate(columns, axis=0) - low
    lane = lax.broadcasted_iota(jnp.int32, (256, 128), 1)
    return jnp.concatenate(
        [jnp.where(column == lane + b, 1.0, 0.0).astype(BF16) for b in range(0, width, 128)],
        axis=1,
    )


def to_tiles(block):
    return jnp.concatenate([block[:, a : a + 128].reshape(16, 16, 128) for a in (0, 128)], axis=0)


def kernel(
    n_pt,
    n_case,
    n_x,
    n_y,
    points,
    cotangent,
    to_hilbert,
    from_hilbert,
    ln_gain,
    ln_bias,
    w_qkv_in,
    b_qkv,
    w_out_in,
    b_out,
    output,
    grad_points,
    sums1,
    sums2,
    to_s,
    from_s,
    gain_s,
    bias_s,
    b_qkv_s,
    b_out_s,
    w_qkv,
    w_out,
    point_win,
    cot_win,
    out_win,
    grad_win,
    hilbert_p,
    hilbert_c,
    standard_s,
    inverse_s,
    normed_s,
    proj_s,
    d_att_s,
    prob_s,
    attended_t_s,
    d_proj_s,
    vector_s,
    acc1,
    acc2,
    core_send1,
    core_send2,
    core_recv1,
    core_recv2,
    x_send1,
    x_send2,
    x_recv1,
    x_recv2,
    y_send1,
    y_send2,
    y_recv1,
    y_recv2,
    z_recv1,
    z_recv2,
    out_stage,
    grad_stage,
    local_sem,
    ex_send,
    ex_recv,
    ar_send,
    ar_recv,
):
    pt = lax.axis_index("pt")
    case = lax.axis_index("case")
    core = lax.rem(pt, 2)
    member = lax.div(pt, 2)
    x_at = lax.div(member, n_y)
    y_at = lax.rem(member, n_y)
    left = lax.rem(pt + n_pt - 1, n_pt)
    right = lax.rem(pt + 1, n_pt)
    sibling = pt + 1 - 2 * core
    outer = lax.rem(pt + n_pt - 1 + 2 * core, n_pt)

    def x_peer(r):
        to = lax.rem(x_at + r, n_x)
        return to, {"pt": (to * n_y + y_at) * 2 + core, "case": case}

    def y_peer(r):
        to = lax.rem(y_at + r, n_y)
        return to, {"pt": (x_at * n_y + to) * 2 + core, "case": case}

    def z_peer(r):
        to = lax.rem(case + r, n_case)
        return to, {"pt": pt, "case": to}

    def for_peers(peer, count, body):
        def step(r, carry):
            body(*peer(r))
            return carry

        lax.fori_loop(1, count, step, 0)

    barrier = pltpu.get_barrier_semaphore()

    def signal(_, where):
        pl.semaphore_signal(barrier, inc=1, device_id=where, device_id_type=MESH)

    to_sib = {"pt": sibling, "case": case}
    signal(None, {"pt": outer, "case": case})
    signal(None, to_sib)
    loads = [
        (points, point_win.at[pl.ds(HALF, LEN)]),
        (cotangent, cot_win.at[pl.ds(HALF, LEN)]),
        (from_hilbert, from_s),
        (ln_gain, gain_s.at[0]),
        (ln_bias, bias_s.at[0]),
        (w_qkv_in, w_qkv),
        (b_qkv, b_qkv_s.at[0]),
        (w_out_in, w_out),
        (b_out, b_out_s.at[0]),
        (to_hilbert, to_s),
    ]
    loads = [pltpu.make_async_copy(a, b, local_sem.at[i]) for i, (a, b) in enumerate(loads)]
    for load in loads:
        load.start()
    for_peers(x_peer, n_x, signal)
    for_peers(y_peer, n_y, signal)
    for_peers(z_peer, n_case, signal)
    pl.semaphore_wait(barrier, 2 + (n_x - 1) + (n_y - 1) + (n_case - 1))

    def remote(src, dst, send_sem, recv_sem, where):
        return pltpu.make_async_remote_copy(
            src_ref=src,
            dst_ref=dst,
            send_sem=send_sem,
            recv_sem=recv_sem,
            device_id=where,
            device_id_type=MESH,
        )

    def to_sides(src, first_row, win, at):
        low = remote(
            src.at[pl.ds(first_row, HALF)],
            win.at[pl.ds(HALF + LEN, HALF)],
            ex_send.at[at],
            ex_recv.at[at],
            {"pt": left, "case": case},
        )
        high = remote(
            src.at[pl.ds(first_row + HALF, HALF)],
            win.at[pl.ds(0, HALF)],
            ex_send.at[at + 1],
            ex_recv.at[at + 1],
            {"pt": right, "case": case},
        )
        low.start()
        high.start()
        return low, high

    ex_p = to_sides(points, 0, point_win, 0)
    ex_c = to_sides(cotangent, 0, cot_win, 2)

    own = pl.ds(HALF, LEN)
    offset = pt * LEN - HALF

    def patch(p):
        return pl.ds(p * PATCH, PATCH)

    for load in loads[:3]:
        load.wait()
    from_row = from_s[...] - offset
    hots = []
    for p in range(2):
        row = from_row[:, p * PATCH : (p + 1) * PATCH]
        hot = one_hot(row, HALF, LEN)
        hilbert_p[patch(p), :] = nn(hot, point_win[own, :])
        hilbert_c[patch(p), :] = nn(hot, cot_win[own, :])
        hots.append(one_hot(row, p * (HALF + LEN), HALF))
    for load in loads[3:]:
        load.wait()

    gain = gain_s[...]
    for p in range(2):
        ex_p[1 - p].wait_recv()
        features = hilbert_p[patch(p), :] + nn(hots[p], point_win[pl.ds(p * (HALF + LEN), HALF), :])
        hilbert_p[patch(p), :] = features
        centered = features - jnp.mean(features, axis=-1, keepdims=True)
        inverse = lax.rsqrt(jnp.mean(centered * centered, axis=-1, keepdims=True) + epsilon)
        standard = centered * inverse
        standard_s[patch(p), :] = standard
        inverse_s[patch(p), :] = jnp.broadcast_to(inverse, (PATCH, 128))
        normed = (standard * gain + bias_s[...]).astype(BF16)
        normed_s[patch(p), :] = normed
        proj_s[patch(p), :] = (nn(normed, w_qkv[...]) + b_qkv_s[...]).astype(BF16)
    for p in range(2):
        ex_c[1 - p].wait_recv()
        cot = hilbert_c[patch(p), :] + nn(hots[p], cot_win[pl.ds(p * (HALF + LEN), HALF), :])
        hilbert_c[patch(p), :] = cot
        d_att_s[patch(p), :] = nt(cot.astype(BF16), w_out[...]).astype(BF16)

    lane_head = lax.broadcasted_iota(jnp.int32, (1, 128), 1) // HEAD
    masks = [jnp.where(lane_head == h, 1.0, 0.0).astype(BF16) for h in range(4)]

    for p in range(2):
        for block in range(2):
            b0 = block * 128
            q = proj_s[patch(p), pl.ds(b0, 128)]
            k = proj_s[patch(p), pl.ds(256 + b0, 128)]
            v_t = jnp.transpose(proj_s[patch(p), pl.ds(512 + b0, 128)])
            da = d_att_s[patch(p), pl.ds(b0, 128)]
            d_v = None
            for h in range(4):
                mask = masks[h]
                exponent = jnp.exp2(nt(k * mask, q) * EXP2_SCALE)
                total = jnp.sum(exponent, axis=0, keepdims=True)
                prob = exponent * (1.0 / total)
                prob_s[(p * 2 + block) * 4 + h] = prob
                prob_low = prob.astype(BF16)
                att_t = nn(v_t[h * HEAD : (h + 1) * HEAD], prob_low)
                attended_t_s[pl.ds(b0 + h * HEAD, HEAD), patch(p)] = att_t.astype(BF16)
                d_v_h = nn(prob_low, da * mask)
                d_v = d_v_h if d_v is None else d_v + d_v_h
            d_proj_s[patch(p), pl.ds(512 + b0, 128)] = d_v.astype(BF16)

    chunks = (
        (acc1, core_send1, core_recv1, x_send1, x_recv1, y_send1, y_recv1, z_recv1, sums1),
        (acc2, core_send2, core_recv2, x_send2, x_recv2, y_send2, y_recv2, z_recv2, sums2),
    )
    per_x = TILES // n_x
    per_y = per_x // n_y

    def sem(chunk, stage):
        return ar_send.at[chunk * 7 + stage], ar_recv.at[chunk * 7 + stage]

    def wait_total(ref, semaphore):
        pltpu.make_async_copy(ref, ref, semaphore).wait()

    def high_low(value):
        high = value.astype(BF16)
        low = (value - high.astype(F32)).astype(BF16)
        return jnp.concatenate([high, low], axis=0)

    def joined(tile):
        tile = tile.astype(F32)
        return tile[:8] + tile[8:]

    def core_start(chunk, first, second):
        acc, send, recv = chunks[chunk][:3]
        acc[0] = to_tiles(first)
        acc[1] = to_tiles(second)
        send[pl.ds(0, TILES)] = acc[1 - core].astype(BF16)
        if chunk:
            theirs = pl.multiple_of((1 - core) * 8, 8)
            send[TILES] = high_low(vector_s[pl.ds(theirs, 8), :])
        copy = remote(send, recv, *sem(chunk, 0), to_sib)
        copy.start()
        return copy

    def x_start(chunk, copy):
        acc, _, recv0, send, recv = chunks[chunk][:5]
        copy.wait()
        half = (acc[core] + recv0[pl.ds(0, TILES)].astype(F32)).astype(BF16)
        send[:, pl.ds(0, per_x)] = half.reshape(n_x, per_x, 16, 128)
        if chunk:
            mine = pl.multiple_of(core * 8, 8)
            tile = high_low(vector_s[pl.ds(mine, 8), :] + joined(recv0[TILES]))
            for i in range(n_x):
                send[i, per_x] = tile
        recv[pl.ds(x_at, 1)] = send[pl.ds(x_at, 1)]
        s, r = sem(chunk, 1)
        for_peers(
            x_peer,
            n_x,
            lambda to, where: remote(send.at[to], recv.at[x_at], s, r, where).start(),
        )

    def y_start(chunk):
        recv0, send, recv = chunks[chunk][4:7]
        wait_total(recv0.at[pl.ds(0, n_x - 1)], sem(chunk, 1)[1])
        part = jnp.sum(recv0[:, pl.ds(0, per_x)].astype(F32), axis=0).astype(BF16)
        send[:, pl.ds(0, per_y)] = part.reshape(n_y, per_y, 16, 128)
        if chunk:
            total = joined(recv0[0, per_x])
            for i in range(1, n_x):
                total = total + joined(recv0[i, per_x])
            tile = high_low(total)
            for i in range(n_y):
                send[i, per_y] = tile
        recv[pl.ds(y_at, 1)] = send[pl.ds(y_at, 1)]
        s, r = sem(chunk, 2)
        for_peers(
            y_peer,
            n_y,
            lambda to, where: remote(send.at[to], recv.at[y_at], s, r, where).start(),
        )

    def z_start(chunk):
        recv0, recv = chunks[chunk][6:8]
        wait_total(recv0.at[pl.ds(0, n_y - 1)], sem(chunk, 2)[1])
        part = jnp.sum(recv0[:, pl.ds(0, per_y)].astype(F32), axis=0).astype(BF16)
        recv[case, pl.ds(0, per_y)] = part
        if chunk:
            total = joined(recv0[0, per_y])
            for i in range(1, n_y):
                total = total + joined(recv0[i, per_y])
            recv[case, per_y] = high_low(total)
        s, r = sem(chunk, 3)
        slot = recv.at[case]
        for_peers(z_peer, n_case, lambda to, where: remote(slot, slot, s, r, where).start())

    def y_back(chunk):
        recv0, result = chunks[chunk][7:9]
        wait_total(recv0.at[pl.ds(0, n_case - 1)], sem(chunk, 3)[1])
        at = pl.ds(x_at * per_x + y_at * per_y, per_y)
        result[core, at] = jnp.sum(recv0[:, pl.ds(0, per_y)].astype(F32), axis=0).astype(BF16)
        if chunk:
            total = joined(recv0[0, per_y])
            for i in range(1, n_case):
                total = total + joined(recv0[i, per_y])
            result[core, TILES] = high_low(total)
        s, r = sem(chunk, 4)
        slot = result.at[core, at]
        for_peers(y_peer, n_y, lambda to, where: remote(slot, slot, s, r, where).start())

    def x_back(chunk):
        result = chunks[chunk][8]
        wait_total(result.at[core, pl.ds(0, (n_y - 1) * per_y)], sem(chunk, 4)[1])
        s, r = sem(chunk, 5)
        slot = result.at[core, pl.ds(x_at * per_x, per_x)]
        for_peers(x_peer, n_x, lambda to, where: remote(slot, slot, s, r, where).start())

    def core_back(chunk):
        result = chunks[chunk][8]
        wait_total(result.at[core, pl.ds(0, (n_x - 1) * per_x)], sem(chunk, 5)[1])
        slot = result.at[core]
        copy = remote(slot, slot, *sem(chunk, 6), to_sib)
        copy.start()
        return copy

    def finish(chunk, copy):
        _, _, _, send1, _, send2, _, recv3, result = chunks[chunk]
        wait_total(send1.at[pl.ds(0, n_x - 1)], sem(chunk, 1)[0])
        wait_total(send2.at[pl.ds(0, n_y - 1)], sem(chunk, 2)[0])
        wait_total(recv3.at[pl.ds(0, n_case - 1)], sem(chunk, 3)[0])
        wait_total(result.at[core, pl.ds(0, (n_y - 1) * per_y)], sem(chunk, 4)[0])
        wait_total(result.at[core, pl.ds(0, (n_x - 1) * per_x)], sem(chunk, 5)[0])
        copy.wait()

    normed_t = jnp.transpose(normed_s[...])
    cot_low = hilbert_c[...].astype(BF16)
    core_copy1 = core_start(
        0, nn(normed_t, d_proj_s[:, pl.ds(512, 256)]), nn(attended_t_s[...], cot_low)
    )

    for p in range(2):
        attended = jnp.transpose(attended_t_s[:, patch(p)])
        branch = nn(attended, w_out[...]) + b_out_s[...]
        out_win[pl.ds(HALF + p * PATCH, PATCH), :] = (hilbert_p[patch(p), :] + branch).astype(BF16)
    ex_out = to_sides(out_win, HALF, out_win, 4)

    for p in range(2):
        for block in range(2):
            b0 = block * 128
            q = proj_s[patch(p), pl.ds(b0, 128)]
            k_t = jnp.transpose(proj_s[patch(p), pl.ds(256 + b0, 128)])
            v = proj_s[patch(p), pl.ds(512 + b0, 128)]
            da = d_att_s[patch(p), pl.ds(b0, 128)]
            d_q_t = []
            d_k = None
            for h in range(4):
                mask = masks[h]
                prob = prob_s[(p * 2 + block) * 4 + h]
                d_prob = nt(v * mask, da)
                row_sum = jnp.sum(prob * d_prob, axis=0, keepdims=True)
                d_s = (prob * (d_prob - row_sum) * SCALE).astype(BF16)
                d_k_h = nn(d_s, q * mask)
                d_k = d_k_h if d_k is None else d_k + d_k_h
                d_q_t.append(nn(k_t[h * HEAD : (h + 1) * HEAD], d_s))
            d_q = jnp.transpose(jnp.concatenate(d_q_t, axis=0))
            d_proj_s[patch(p), pl.ds(b0, 128)] = d_q.astype(BF16)
            d_proj_s[patch(p), pl.ds(256 + b0, 128)] = d_k.astype(BF16)
        if p == 0:
            x_start(0, core_copy1)
        else:
            y_start(0)

    d_proj = d_proj_s[...]
    d_normed = nt(d_proj, w_qkv[...])
    standard = standard_s[...]
    cot_all = hilbert_c[...]
    vector_s[...] = jnp.zeros((16, 128), F32)
    b_sum = jnp.sum(d_proj.astype(F32), axis=0, keepdims=True)
    for part in range(6):
        vector_s[part : part + 1, :] = b_sum[:, part * 128 : part * 128 + 128]
    rest = (
        jnp.sum(cot_all, axis=0, keepdims=True),
        jnp.sum(d_normed * standard, axis=0, keepdims=True),
        jnp.sum(d_normed, axis=0, keepdims=True),
    )
    for i, value in enumerate(rest):
        for part in range(2):
            vector_s[8 + 2 * i + part : 9 + 2 * i + part, :] = value[:, part * 128 : part * 128 + 128]
    core_copy2 = core_start(1, nn(normed_t, d_proj[:, :256]), nn(normed_t, d_proj[:, 256:512]))

    scaled = d_normed * gain
    inverse = inverse_s[...]
    inverse = jnp.concatenate([inverse, inverse], axis=1)
    d_input = inverse * (
        scaled
        - jnp.mean(scaled, axis=-1, keepdims=True)
        - standard * jnp.mean(scaled * standard, axis=-1, keepdims=True)
    )
    grad_win[own, :] = (cot_all + d_input).astype(BF16)
    ex_grad = to_sides(grad_win, HALF, grad_win, 6)

    to_row = to_s[...] - offset

    def to_z_order(pair, win, stage, result, at):
        for copy in pair:
            copy.wait_recv()
        for p in range(2):
            hot = one_hot(to_row[:, p * PATCH : (p + 1) * PATCH], p * HALF, HALF + LEN)
            stage[patch(p), :] = nn(hot, win[pl.ds(p * HALF, HALF + LEN), :]).astype(BF16)
        store = pltpu.make_async_copy(stage, result, local_sem.at[at])
        store.start()
        return store

    x_start(1, core_copy2)
    z_start(0)
    store_out = to_z_order(ex_out, out_win, out_stage, output, 10)
    y_start(1)
    y_back(0)
    store_grad = to_z_order(ex_grad, grad_win, grad_stage, grad_points, 11)
    z_start(1)
    x_back(0)
    y_back(1)
    last1 = core_back(0)
    x_back(1)
    last2 = core_back(1)
    finish(0, last1)
    for pair in (ex_p, ex_c, ex_out, ex_grad):
        for copy in pair:
            copy.wait_send()
    store_out.wait()
    store_grad.wait()
    finish(1, last2)


def results_kernel(
    factor,
    output_in,
    grad_in,
    sums1,
    sums2,
    output,
    grad_points,
    grad_w_qkv,
    grad_b_qkv,
    grad_w_out,
    grad_b_out,
    grad_gain,
    grad_bias,
    vec_s,
    sems,
):
    copies = [
        pltpu.make_async_copy(output_in, output, sems.at[0]),
        pltpu.make_async_copy(grad_in, grad_points, sems.at[1]),
    ]
    for copy in copies:
        copy.start()
    vectors = []
    for c in range(2):
        tile = sums2[c, TILES].astype(F32)
        vectors.append((tile[:8] + tile[8:]) * factor)
    for part in range(6):
        vec_s[0:1, part * 128 : part * 128 + 128] = vectors[0][part : part + 1]
        row = 1 + part // 2
        vec_s[row : row + 1, (part % 2) * 128 : (part % 2) * 128 + 128] = vectors[1][part : part + 1]
    small = [
        pltpu.make_async_copy(vec_s.at[0], grad_b_qkv, sems.at[2]),
        pltpu.make_async_copy(vec_s.at[1, pl.ds(0, D)], grad_b_out, sems.at[3]),
        pltpu.make_async_copy(vec_s.at[2, pl.ds(0, D)], grad_gain, sems.at[4]),
        pltpu.make_async_copy(vec_s.at[3, pl.ds(0, D)], grad_bias, sems.at[5]),
    ]
    for copy in small:
        copy.start()

    def block(sums, c, half):
        return sums[c, pl.ds(half * 16, 16)].reshape(256, 128).astype(F32) * factor

    for half in range(2):
        lanes = half * 128
        grad_w_qkv[:, pl.ds(lanes, 128)] = block(sums2, 0, half)
        grad_w_qkv[:, pl.ds(256 + lanes, 128)] = block(sums2, 1, half)
        grad_w_qkv[:, pl.ds(512 + lanes, 128)] = block(sums1, 0, half)
        grad_w_out[:, pl.ds(lanes, 128)] = block(sums1, 1, half)
    for copy in copies + small:
        copy.wait()


def on_device(n_pt, n_case, n_x, n_y, points, cotangent, to_hilbert, from_hilbert, *params):
    per_x = TILES // n_x
    per_y = per_x // n_y
    vmem = pl.BlockSpec(memory_space=pltpu.VMEM)
    hbm = pl.BlockSpec(memory_space=pl.ANY)
    shape = jax.ShapeDtypeStruct
    rows = shape((LEN, D), BF16)

    def tiles(*lead):
        return pltpu.VMEM((*lead, 16, 128), BF16)

    output, grad_points, sums1, sums2 = pl.pallas_call(
        functools.partial(kernel, n_pt, n_case, n_x, n_y),
        out_shape=(
            rows,
            rows,
            shape((2, TILES, 16, 128), BF16),
            shape((2, TILES + 1, 16, 128), BF16),
        ),
        in_specs=[hbm] * 10,
        out_specs=(hbm, hbm, vmem, vmem),
        scratch_shapes=[
            pltpu.VMEM((1, LEN), jnp.int32),
            pltpu.VMEM((1, LEN), jnp.int32),
            pltpu.VMEM((1, D), F32),
            pltpu.VMEM((1, D), F32),
            pltpu.VMEM((1, 3 * D), F32),
            pltpu.VMEM((1, D), F32),
            pltpu.VMEM((D, 3 * D), BF16),
            pltpu.VMEM((D, D), BF16),
            pltpu.VMEM((WIN, D), BF16),
            pltpu.VMEM((WIN, D), BF16),
            pltpu.VMEM((WIN, D), BF16),
            pltpu.VMEM((WIN, D), BF16),
            pltpu.VMEM((LEN, D), F32),
            pltpu.VMEM((LEN, D), F32),
            pltpu.VMEM((LEN, D), F32),
            pltpu.VMEM((LEN, 128), F32),
            pltpu.VMEM((LEN, D), BF16),
            pltpu.VMEM((LEN, 3 * D), BF16),
            pltpu.VMEM((LEN, D), BF16),
            pltpu.VMEM((16, PATCH, PATCH), F32),
            pltpu.VMEM((D, LEN), BF16),
            pltpu.VMEM((LEN, 3 * D), BF16),
            pltpu.VMEM((16, 128), F32),
            pltpu.VMEM((2, TILES, 16, 128), F32),
            pltpu.VMEM((2, TILES, 16, 128), F32),
            tiles(TILES),
            tiles(TILES + 1),
            tiles(TILES),
            tiles(TILES + 1),
            tiles(n_x, per_x),
            tiles(n_x, per_x + 1),
            tiles(n_x, per_x),
            tiles(n_x, per_x + 1),
            tiles(n_y, per_y),
            tiles(n_y, per_y + 1),
            tiles(n_y, per_y),
            tiles(n_y, per_y + 1),
            tiles(n_case, per_y),
            tiles(n_case, per_y + 1),
            pltpu.VMEM((LEN, D), BF16),
            pltpu.VMEM((LEN, D), BF16),
            pltpu.SemaphoreType.DMA((12,)),
            pltpu.SemaphoreType.DMA((8,)),
            pltpu.SemaphoreType.DMA((8,)),
            pltpu.SemaphoreType.DMA((14,)),
            pltpu.SemaphoreType.DMA((14,)),
        ],
        compiler_params=pltpu.CompilerParams(
            collective_id=0, has_side_effects=True, vmem_limit_bytes=VMEM_LIMIT
        ),
    )(points[0], cotangent[0], to_hilbert, from_hilbert, *params)
    factor = 1.0 / math.sqrt(n_pt * n_case * LEN)
    result = pl.pallas_call(
        functools.partial(results_kernel, factor),
        out_shape=(
            rows,
            rows,
            shape((D, 3 * D), F32),
            shape((3 * D,), F32),
            shape((D, D), F32),
            shape((D,), F32),
            shape((D,), F32),
            shape((D,), F32),
        ),
        in_specs=[vmem] * 4,
        out_specs=(hbm, hbm, vmem, hbm, vmem, hbm, hbm, hbm),
        scratch_shapes=[pltpu.VMEM((4, 3 * D), F32), pltpu.SemaphoreType.DMA((6,))],
        compiler_params=pltpu.CompilerParams(vmem_limit_bytes=VMEM_LIMIT),
    )(output, grad_points, sums1, sums2)
    return (result[0][None], result[1][None], *result[2:])


def solution(mesh):
    n_pt, n_case = mesh.shape["pt"], mesh.shape["case"]
    members = n_pt // 2
    n_y = 8 if members >= 32 else 2
    rows = P("case", "pt", None)
    index = P("case", "pt")
    return jax.shard_map(
        functools.partial(on_device, n_pt, n_case, members // n_y, n_y),
        mesh=mesh,
        in_specs=(rows, rows, index, index) + (P(),) * 6,
        out_specs=(rows, rows) + (P(),) * 6,
        check_vma=False,
    )
```

time: 541 us -> 64 us (0.12)
  the two profiles are of different devices: /device:TPU:23 before, /device:TPU:1 now
where the time goes in v1:
time: 64 us; the launch traced here: 63.8 us
  Pallas kernels  63.2 us (99%)
  between operations  0.64 us (1%)
    pallas_call x1, Pallas kernels, on_device(): pl.pallas_call(functools.partial(kernel, n_pt, n_case, n_x, n_y), out_sha...  60.2 us
    pallas_call x1, Pallas kernels, on_device(): pl.pallas_call(functools.partial(results_kernel, factor), out_shape=(rows...  3 us

profile of v1, /device:TPU:1, one launch (start us, length us, event | category | flops | bytes accessed | tf_op | source)
XLA Modules:
  0.0 63.8 jit_solution(15967282349466153997)
XLA Ops:
  0.6 60.2 %shard_map.161 = (bf16[512,256]{1,0:T(8,128)(2,1)}, bf16[512,256]{1,0:T(8,128)(2,1)}, bf16[2,32,16,128]{3,2,1,0:T(8,128)(2,1)}, bf16[2,33,16,128]{3,2,1,0:T(8,128)(2,1)}) custom-call(bf16[512,256]{1,0:T(8,128)(2,1)} %bitcast.4, bf16[512,256]{1,0:T(8,128)(2,1)} %bitcast.5, s32[1,512]{1,0:T(1,128)} %to_hilbert.1, s32[1,512]{1,0:T(1,128)} %from_hilbert.1, ...), custom_call_target="tpu_custom_call" | custom-call | tf_op jit(solution)/shard_map/pallas_call | solution.py:559
  60.8 3.0 %shard_map.162 = (bf16[512,256]{1,0:T(8,128)(2,1)}, bf16[512,256]{1,0:T(8,128)(2,1)}, f32[256,768]{1,0:T(8,128)}, f32[768]{0:T(1024)}, f32[256,256]{1,0:T(8,128)...) custom-call(bf16[512,256]{1,0:T(8,128)(2,1)} %get-tuple-element.20.output_in, bf16[512,256]{1,0:T(8,128)(2,1)} %get-tuple-element.21.grad_in, ...), custom_call_target="tpu_custom_call" | custom-call | tf_op jit(solution)/shard_map/pallas_call | solution.py:622

commit v2 on v1

v2 whole, which is shorter than its diff:
```python
import functools
import math

import jax
import jax.numpy as jnp
from jax import lax
from jax.experimental import pallas as pl
from jax.experimental.pallas import tpu as pltpu
from jax.sharding import PartitionSpec as P

D = 256
HEADS = 8
HEAD = 32
PATCH = 256
LEN = 512
HALF = 256
WIN = 1024
TILES = 32
epsilon = 1e-05
VMEM_LIMIT = 60 * 1024 * 1024
SCALE = 1.0 / math.sqrt(HEAD)
EXP2_SCALE = SCALE * math.log2(math.e)

MESH = pl.DeviceIdType.MESH
F32 = jnp.float32
BF16 = jnp.bfloat16


def nn(a, b):
    return lax.dot_general(a, b, (((1,), (0,)), ((), ())), preferred_element_type=F32)


def nt(a, b):
    return lax.dot_general(a, b, (((1,), (1,)), ((), ())), preferred_element_type=F32)


def one_hot(index_row, low, width):
    columns = [
        jnp.transpose(jnp.broadcast_to(index_row[:, a : a + 128], (128, 128))) for a in (0, 128)
    ]
    column = jnp.concatenate(columns, axis=0) - low
    lane = lax.broadcasted_iota(jnp.int32, (256, 128), 1)
    return jnp.concatenate(
        [jnp.where(column == lane + b, 1.0, 0.0).astype(BF16) for b in range(0, width, 128)],
        axis=1,
    )


def ring_order(n_x, n_y):
    places = [(x, y) for x in range(n_x) for y in range(n_y) if x or y]
    return sorted(places, key=lambda p: -(min(p[0], n_x - p[0]) + min(p[1], n_y - p[1])))


def to_tiles(block):
    return jnp.concatenate([block[:, a : a + 128].reshape(16, 16, 128) for a in (0, 128)], axis=0)


def kernel(
    n_pt,
    n_case,
    n_x,
    n_y,
    points,
    cotangent,
    to_hilbert,
    from_hilbert,
    ln_gain,
    ln_bias,
    w_qkv_in,
    b_qkv,
    w_out_in,
    b_out,
    output,
    grad_points,
    sums1,
    sums2,
    to_s,
    from_s,
    gain_s,
    bias_s,
    b_qkv_s,
    b_out_s,
    w_qkv,
    w_out,
    point_win,
    cot_win,
    out_win,
    grad_win,
    hilbert_p,
    hilbert_c,
    standard_s,
    inverse_s,
    normed_t_s,
    proj_s,
    d_att_s,
    prob_s,
    attended_t_s,
    d_proj_s,
    d_normed_s,
    vector_s,
    acc1,
    acc2,
    core_send1,
    core_send2,
    core_recv1,
    core_recv2,
    m_send1,
    m_send2,
    m_recv1,
    m_recv2,
    z_recv1,
    z_recv2,
    vec_z,
    vec_m,
    out_stage,
    grad_stage,
    local_sem,
    ex_send,
    ex_recv,
    ar_send,
    ar_recv,
    in_sem,
):
    pt = lax.axis_index("pt")
    case = lax.axis_index("case")
    core = lax.rem(pt, 2)
    members = n_pt // 2
    member = lax.div(pt, 2)
    sibling = pt + 1 - 2 * core
    outer = lax.rem(pt + n_pt - 1 + 2 * core, n_pt)

    x_at = lax.div(member, n_y)
    y_at = lax.rem(member, n_y)

    def m_peer(place):
        to = lax.rem(x_at + place[0], n_x) * n_y + lax.rem(y_at + place[1], n_y)
        return to, {"pt": to * 2 + core, "case": case}

    def z_peer(r):
        to = lax.rem(case + r, n_case)
        return to, {"pt": pt, "case": to}

    m_peers = [m_peer(place) for place in ring_order(n_x, n_y)]
    z_peers = [z_peer(r) for _, r in ring_order(1, n_case)]

    def for_peers(peers, body):
        for peer in peers:
            body(*peer)

    barrier = pltpu.get_barrier_semaphore()

    def signal(_, where):
        pl.semaphore_signal(barrier, inc=1, device_id=where, device_id_type=MESH)

    to_sib = {"pt": sibling, "case": case}
    signal(None, {"pt": outer, "case": case})
    signal(None, to_sib)
    loads = [
        (points, point_win.at[pl.ds(HALF, LEN)]),
        (cotangent, cot_win.at[pl.ds(HALF, LEN)]),
        (from_hilbert, from_s),
        (ln_gain, gain_s.at[0]),
        (ln_bias, bias_s.at[0]),
        (w_qkv_in, w_qkv),
        (b_qkv, b_qkv_s.at[0]),
        (w_out_in, w_out),
        (b_out, b_out_s.at[0]),
        (to_hilbert, to_s),
    ]
    loads = [pltpu.make_async_copy(a, b, local_sem.at[i]) for i, (a, b) in enumerate(loads)]
    for load in loads:
        load.start()
    near = [m_peer((0, 1)), m_peer((0, n_y - 1)), m_peer((1, 0)), m_peer((n_x - 1, 0))]
    near += [z_peer(1), z_peer(n_case - 1)]
    for_peers(near, signal)
    pl.semaphore_wait(barrier, 2 + len(near))

    def tell(step, peers):
        for _, where in peers:
            pl.semaphore_signal(in_sem.at[step], inc=1, device_id=where, device_id_type=MESH)

    def heard(step, peers):
        pl.semaphore_wait(in_sem.at[step], len(peers))

    steps = [near]
    if n_y > 4 or n_case > 4:
        steps.append([m_peer((0, 2)), m_peer((0, n_y - 2)), z_peer(2), z_peer(n_case - 2)])
    steps.append([m_peer((dx, 0)) for dx in range(1, n_x)])
    tell(0, steps[0])

    def remote(src, dst, send_sem, recv_sem, where):
        return pltpu.make_async_remote_copy(
            src_ref=src,
            dst_ref=dst,
            send_sem=send_sem,
            recv_sem=recv_sem,
            device_id=where,
            device_id_type=MESH,
        )

    halves = (1 - core, core)

    def rows_of(p, first=0):
        return pl.ds(pl.multiple_of(first + p * PATCH, PATCH), PATCH)

    def side_rows(p):
        return pl.ds(pl.multiple_of(p * (HALF + LEN), HALF), HALF)

    def to_side(i, src, first_row, win, at):
        where = to_sib if i == 0 else {"pt": outer, "case": case}
        p = halves[i]
        copy = remote(
            src.at[rows_of(p, first_row)],
            win.at[side_rows(1 - p)],
            ex_send.at[at + i],
            ex_recv.at[at + i],
            where,
        )
        copy.start()
        return copy

    ex_p = [to_side(i, points, 0, point_win, 0) for i in (1, 0)][::-1]
    ex_c = [to_side(i, cotangent, 0, cot_win, 2) for i in (1, 0)][::-1]
    ex_out = [None, None]
    ex_grad = [None, None]

    own = pl.ds(HALF, LEN)
    offset = pt * LEN - HALF

    for load in loads[:3]:
        load.wait()
    hots = []
    for i, p in enumerate(halves):
        row = from_s[:, rows_of(p)] - offset
        hot = one_hot(row, HALF, LEN)
        hilbert_p[i] = nn(hot, point_win[own, :])
        hilbert_c[i] = nn(hot, cot_win[own, :])
        hots.append(one_hot(row, p * (HALF + LEN), HALF))
    for load in loads[3:]:
        load.wait()
    heard(0, steps[0])
    tell(1, steps[1])

    def heard_rings():
        if len(steps) == 3:
            heard(1, steps[1])
            tell(2, steps[2])

    gain = gain_s[...]
    lane_head = lax.broadcasted_iota(jnp.int32, (1, 128), 1) // HEAD
    masks = [jnp.where(lane_head == h, 1.0, 0.0).astype(BF16) for h in range(4)]

    def project(i):
        p = halves[i]
        ex_p[i].wait_recv()
        features = hilbert_p[i] + nn(hots[i], point_win[side_rows(p), :])
        hilbert_p[i] = features
        centered = features - jnp.mean(features, axis=-1, keepdims=True)
        inverse = lax.rsqrt(jnp.mean(centered * centered, axis=-1, keepdims=True) + epsilon)
        standard = centered * inverse
        standard_s[i] = standard
        inverse_s[i] = jnp.broadcast_to(inverse, (PATCH, 128))
        normed = (standard * gain + bias_s[...]).astype(BF16)
        normed_t_s[i] = jnp.transpose(normed)
        proj_s[i] = (nn(normed, w_qkv[...]) + b_qkv_s[...]).astype(BF16)
        ex_c[i].wait_recv()
        cot = hilbert_c[i] + nn(hots[i], cot_win[side_rows(p), :])
        hilbert_c[i] = cot
        d_att_s[i] = nt(cot.astype(BF16), w_out[...]).astype(BF16)

    def first_pass(i):
        for block in range(2):
            b0 = block * 128
            q = proj_s[i, :, pl.ds(b0, 128)]
            k = proj_s[i, :, pl.ds(256 + b0, 128)]
            v_t = jnp.transpose(proj_s[i, :, pl.ds(512 + b0, 128)])
            da = d_att_s[i, :, pl.ds(b0, 128)]
            d_v = None
            for h in range(4):
                mask = masks[h]
                exponent = jnp.exp2(nt(k * mask, q) * EXP2_SCALE)
                total = jnp.sum(exponent, axis=0, keepdims=True)
                prob = exponent * (1.0 / total)
                prob_s[block * 4 + h] = prob
                prob_low = prob.astype(BF16)
                att_t = nn(v_t[h * HEAD : (h + 1) * HEAD], prob_low)
                attended_t_s[i, pl.ds(b0 + h * HEAD, HEAD), :] = att_t.astype(BF16)
                d_v_h = nn(prob_low, da * mask)
                d_v = d_v_h if d_v is None else d_v + d_v_h
            d_proj_s[i, :, pl.ds(512 + b0, 128)] = d_v.astype(BF16)

    def block_output(i):
        attended = jnp.transpose(attended_t_s[i])
        branch = nn(attended, w_out[...]) + b_out_s[...]
        out_win[rows_of(halves[i], HALF), :] = (hilbert_p[i] + branch).astype(BF16)
        ex_out[i] = to_side(i, out_win, HALF, out_win, 4)

    def second_pass(i, block):
        b0 = block * 128
        q = proj_s[i, :, pl.ds(b0, 128)]
        k_t = jnp.transpose(proj_s[i, :, pl.ds(256 + b0, 128)])
        v = proj_s[i, :, pl.ds(512 + b0, 128)]
        da = d_att_s[i, :, pl.ds(b0, 128)]
        d_q_t = []
        d_k = None
        for h in range(4):
            mask = masks[h]
            prob = prob_s[block * 4 + h]
            d_prob = nt(v * mask, da)
            row_sum = jnp.sum(prob * d_prob, axis=0, keepdims=True)
            d_s = (prob * (d_prob - row_sum) * SCALE).astype(BF16)
            d_k_h = nn(d_s, q * mask)
            d_k = d_k_h if d_k is None else d_k + d_k_h
            d_q_t.append(nn(k_t[h * HEAD : (h + 1) * HEAD], d_s))
        d_q = jnp.transpose(jnp.concatenate(d_q_t, axis=0))
        d_proj_s[i, :, pl.ds(b0, 128)] = d_q.astype(BF16)
        d_proj_s[i, :, pl.ds(256 + b0, 128)] = d_k.astype(BF16)

    def add(ref, index, value, i):
        ref[index] = value if i == 0 else ref[index] + value

    def forward_terms(i):
        d_v = d_proj_s[i, :, pl.ds(512, 256)]
        add(acc1, 0, to_tiles(nn(normed_t_s[i], d_v)), i)
        add(acc1, 1, to_tiles(nn(attended_t_s[i], hilbert_c[i].astype(BF16))), i)

    def backward_terms(i):
        d_proj = d_proj_s[i]
        d_normed = nt(d_proj, w_qkv[...])
        d_normed_s[...] = d_normed
        sums = (
            (0, jnp.sum(d_proj.astype(F32), axis=0, keepdims=True)),
            (8, jnp.sum(hilbert_c[i], axis=0, keepdims=True)),
            (10, jnp.sum(d_normed * standard_s[i], axis=0, keepdims=True)),
            (12, jnp.sum(d_normed, axis=0, keepdims=True)),
        )
        if i == 0:
            vector_s[...] = jnp.zeros((16, 128), F32)
        for row, value in sums:
            for part in range(value.shape[1] // 128):
                add(
                    vector_s,
                    slice(row + part, row + part + 1),
                    value[:, part * 128 : part * 128 + 128],
                    i,
                )
        add(acc2, 0, to_tiles(nn(normed_t_s[i], d_proj[:, :256])), i)
        add(acc2, 1, to_tiles(nn(normed_t_s[i], d_proj[:, 256:512])), i)

    def norm_backward(i):
        d_normed = d_normed_s[...]
        standard = standard_s[i]
        scaled = d_normed * gain
        inverse = inverse_s[i]
        inverse = jnp.concatenate([inverse, inverse], axis=1)
        d_input = inverse * (
            scaled
            - jnp.mean(scaled, axis=-1, keepdims=True)
            - standard * jnp.mean(scaled * standard, axis=-1, keepdims=True)
        )
        grad_win[rows_of(halves[i], HALF), :] = (hilbert_c[i] + d_input).astype(BF16)
        ex_grad[i] = to_side(i, grad_win, HALF, grad_win, 6)

    chunks = (
        (acc1, core_send1, core_recv1, m_send1, m_recv1, z_recv1, sums1),
        (acc2, core_send2, core_recv2, m_send2, m_recv2, z_recv2, sums2),
    )
    per = TILES // members

    def sem(chunk, stage):
        return ar_send.at[chunk * 5 + stage], ar_recv.at[chunk * 5 + stage]

    def wait_total(ref, semaphore):
        pltpu.make_async_copy(ref, ref, semaphore).wait()

    def high_low(value):
        high = value.astype(BF16)
        low = (value - high.astype(F32)).astype(BF16)
        return jnp.concatenate([high, low], axis=0)

    def joined(tile):
        tile = tile.astype(F32)
        return tile[:8] + tile[8:]

    def core_start(chunk):
        acc, send, recv = chunks[chunk][:3]
        send[pl.ds(0, TILES)] = acc[1 - core].astype(BF16)
        if chunk:
            theirs = pl.multiple_of((1 - core) * 8, 8)
            send[TILES] = high_low(vector_s[pl.ds(theirs, 8), :])
        copy = remote(send, recv, *sem(chunk, 0), to_sib)
        copy.start()
        return copy

    def m_start(chunk, copy):
        acc, _, recv0, send, recv = chunks[chunk][:5]
        if chunk == 0:
            copy.wait()
        half = (acc[core] + recv0[pl.ds(0, TILES)].astype(F32)).astype(BF16)
        send[...] = half.reshape(members, per, 16, 128)
        recv[pl.ds(member, 1)] = send[pl.ds(member, 1)]
        s, r = sem(chunk, 1)
        for_peers(
            m_peers,
            lambda to, where: remote(send.at[to], recv.at[member], s, r, where).start(),
        )

    def z_start(chunk):
        recv0, recv = chunks[chunk][4:6]
        wait_total(recv0.at[pl.ds(0, members - 1)], sem(chunk, 1)[1])
        recv[case] = jnp.sum(recv0[...].astype(F32), axis=0).astype(BF16)
        s, r = sem(chunk, 2)
        slot = recv.at[case]
        for_peers(z_peers, lambda to, where: remote(slot, slot, s, r, where).start())

    def m_back(chunk):
        recv0, result = chunks[chunk][5:7]
        wait_total(recv0.at[pl.ds(0, n_case - 1)], sem(chunk, 2)[1])
        at = pl.ds(member * per, per)
        result[core, at] = jnp.sum(recv0[...].astype(F32), axis=0).astype(BF16)
        s, r = sem(chunk, 3)
        slot = result.at[core, at]
        for_peers(m_peers, lambda to, where: remote(slot, slot, s, r, where).start())

    def core_back(chunk):
        result = chunks[chunk][6]
        wait_total(result.at[core, pl.ds(0, (members - 1) * per)], sem(chunk, 3)[1])
        slot = result.at[core, pl.ds(0, TILES)]
        copy = remote(slot, slot, *sem(chunk, 4), to_sib)
        copy.start()
        return copy

    def vec_z_start(copy):
        copy.wait()
        mine = pl.multiple_of(core * 8, 8)
        vec_z[case] = high_low(vector_s[pl.ds(mine, 8), :] + joined(core_recv2[TILES]))
        slot = vec_z.at[case]
        for_peers(
            z_peers,
            lambda to, where: remote(slot, slot, ar_send.at[10], ar_recv.at[10], where).start(),
        )

    def vec_m_start():
        wait_total(vec_z.at[pl.ds(0, n_case - 1)], ar_recv.at[10])
        total = joined(vec_z[0])
        for i in range(1, n_case):
            total = total + joined(vec_z[i])
        vec_m[member] = high_low(total)
        slot = vec_m.at[member]
        for_peers(
            m_peers,
            lambda to, where: remote(slot, slot, ar_send.at[11], ar_recv.at[11], where).start(),
        )

    def vec_back():
        wait_total(vec_m.at[pl.ds(0, members - 1)], ar_recv.at[11])
        total = vec_m[...].astype(F32)
        total = jnp.sum(total, axis=0)
        sums2[core, TILES] = high_low(total[:8] + total[8:])
        slot = sums2.at[core, TILES]
        copy = remote(slot, slot, ar_send.at[12], ar_recv.at[12], to_sib)
        copy.start()
        return copy

    def finish(chunk, copy):
        send1, _, recv2, result = chunks[chunk][3:7]
        wait_total(send1.at[pl.ds(0, members - 1)], sem(chunk, 1)[0])
        wait_total(recv2.at[pl.ds(0, n_case - 1)], sem(chunk, 2)[0])
        wait_total(result.at[core, pl.ds(0, (members - 1) * per)], sem(chunk, 3)[0])
        copy.wait()

    project(0)
    first_pass(0)
    block_output(0)
    heard_rings()
    second_pass(0, 0)
    second_pass(0, 1)
    forward_terms(0)
    backward_terms(0)
    norm_backward(0)
    project(1)
    heard(len(steps) - 1, steps[-1])
    first_pass(1)
    forward_terms(1)
    core_copy1 = core_start(0)
    block_output(1)
    second_pass(1, 0)
    m_start(0, core_copy1)
    second_pass(1, 1)
    backward_terms(1)
    core_copy2 = core_start(1)
    norm_backward(1)

    def to_z_order(pair, win, stage, result, at):
        for copy in pair:
            copy.wait_recv()
        for p in range(2):
            row = to_s[:, p * PATCH : (p + 1) * PATCH] - offset
            hot = one_hot(row, p * HALF, HALF + LEN)
            at_p = pl.ds(p * PATCH, PATCH)
            stage[at_p, :] = nn(hot, win[pl.ds(p * HALF, HALF + LEN), :]).astype(BF16)
        store = pltpu.make_async_copy(stage, result, local_sem.at[at])
        store.start()
        return store

    vec_z_start(core_copy2)
    m_start(1, None)
    z_start(0)
    store_out = to_z_order(ex_out, out_win, out_stage, output, 10)
    vec_m_start()
    m_back(0)
    z_start(1)
    store_grad = to_z_order(ex_grad, grad_win, grad_stage, grad_points, 11)
    m_back(1)
    last1 = core_back(0)
    vec_last = vec_back()
    last2 = core_back(1)
    finish(0, last1)
    wait_total(vec_z.at[pl.ds(0, n_case - 1)], ar_send.at[10])
    wait_total(vec_m.at[pl.ds(0, members - 1)], ar_send.at[11])
    for pair in (ex_p, ex_c, ex_out, ex_grad):
        for copy in pair:
            copy.wait_send()
    store_out.wait()
    store_grad.wait()
    vec_last.wait()
    finish(1, last2)


def results_kernel(
    factor,
    output_in,
    grad_in,
    sums1,
    sums2,
    output,
    grad_points,
    grad_w_qkv,
    grad_b_qkv,
    grad_w_out,
    grad_b_out,
    grad_gain,
    grad_bias,
    vec_s,
    sems,
):
    copies = [
        pltpu.make_async_copy(output_in, output, sems.at[0]),
        pltpu.make_async_copy(grad_in, grad_points, sems.at[1]),
    ]
    for copy in copies:
        copy.start()
    vectors = []
    for c in range(2):
        tile = sums2[c, TILES].astype(F32)
        vectors.append((tile[:8] + tile[8:]) * factor)
    for part in range(6):
        vec_s[0:1, part * 128 : part * 128 + 128] = vectors[0][part : part + 1]
        row = 1 + part // 2
        vec_s[row : row + 1, (part % 2) * 128 : (part % 2) * 128 + 128] = vectors[1][part : part + 1]
    small = [
        pltpu.make_async_copy(vec_s.at[0], grad_b_qkv, sems.at[2]),
        pltpu.make_async_copy(vec_s.at[1, pl.ds(0, D)], grad_b_out, sems.at[3]),
        pltpu.make_async_copy(vec_s.at[2, pl.ds(0, D)], grad_gain, sems.at[4]),
        pltpu.make_async_copy(vec_s.at[3, pl.ds(0, D)], grad_bias, sems.at[5]),
    ]
    for copy in small:
        copy.start()

    def block(sums, c, half):
        return sums[c, pl.ds(half * 16, 16)].reshape(256, 128).astype(F32) * factor

    for half in range(2):
        lanes = half * 128
        grad_w_qkv[:, pl.ds(lanes, 128)] = block(sums2, 0, half)
        grad_w_qkv[:, pl.ds(256 + lanes, 128)] = block(sums2, 1, half)
        grad_w_qkv[:, pl.ds(512 + lanes, 128)] = block(sums1, 0, half)
        grad_w_out[:, pl.ds(lanes, 128)] = block(sums1, 1, half)
    for copy in copies + small:
        copy.wait()


def on_device(n_pt, n_case, n_x, n_y, points, cotangent, to_hilbert, from_hilbert, *params):
    members = n_pt // 2
    per = TILES // members
    vmem = pl.BlockSpec(memory_space=pltpu.VMEM)
    hbm = pl.BlockSpec(memory_space=pl.ANY)
    shape = jax.ShapeDtypeStruct
    rows = shape((LEN, D), BF16)

    def tiles(*lead):
        return pltpu.VMEM((*lead, 16, 128), BF16)

    output, grad_points, sums1, sums2 = pl.pallas_call(
        functools.partial(kernel, n_pt, n_case, n_x, n_y),
        out_shape=(
            rows,
            rows,
            shape((2, TILES, 16, 128), BF16),
            shape((2, TILES + 1, 16, 128), BF16),
        ),
        in_specs=[hbm] * 10,
        out_specs=(hbm, hbm, vmem, vmem),
        scratch_shapes=[
            pltpu.VMEM((1, LEN), jnp.int32),
            pltpu.VMEM((1, LEN), jnp.int32),
            pltpu.VMEM((1, D), F32),
            pltpu.VMEM((1, D), F32),
            pltpu.VMEM((1, 3 * D), F32),
            pltpu.VMEM((1, D), F32),
            pltpu.VMEM((D, 3 * D), BF16),
            pltpu.VMEM((D, D), BF16),
            pltpu.VMEM((WIN, D), BF16),
            pltpu.VMEM((WIN, D), BF16),
            pltpu.VMEM((WIN, D), BF16),
            pltpu.VMEM((WIN, D), BF16),
            pltpu.VMEM((2, PATCH, D), F32),
            pltpu.VMEM((2, PATCH, D), F32),
            pltpu.VMEM((2, PATCH, D), F32),
            pltpu.VMEM((2, PATCH, 128), F32),
            pltpu.VMEM((2, D, PATCH), BF16),
            pltpu.VMEM((2, PATCH, 3 * D), BF16),
            pltpu.VMEM((2, PATCH, D), BF16),
            pltpu.VMEM((8, PATCH, PATCH), F32),
            pltpu.VMEM((2, D, PATCH), BF16),
            pltpu.VMEM((2, PATCH, 3 * D), BF16),
            pltpu.VMEM((PATCH, D), F32),
            pltpu.VMEM((16, 128), F32),
            pltpu.VMEM((2, TILES, 16, 128), F32),
            pltpu.VMEM((2, TILES, 16, 128), F32),
            tiles(TILES),
            tiles(TILES + 1),
            tiles(TILES),
            tiles(TILES + 1),
            tiles(members, per),
            tiles(members, per),
            tiles(members, per),
            tiles(members, per),
            tiles(n_case, per),
            tiles(n_case, per),
            tiles(n_case),
            tiles(members),
            pltpu.VMEM((LEN, D), BF16),
            pltpu.VMEM((LEN, D), BF16),
            pltpu.SemaphoreType.DMA((12,)),
            pltpu.SemaphoreType.DMA((8,)),
            pltpu.SemaphoreType.DMA((8,)),
            pltpu.SemaphoreType.DMA((14,)),
            pltpu.SemaphoreType.DMA((14,)),
            pltpu.SemaphoreType.REGULAR((3,)),
        ],
        compiler_params=pltpu.CompilerParams(
            collective_id=0, has_side_effects=True, vmem_limit_bytes=VMEM_LIMIT
        ),
    )(points[0], cotangent[0], to_hilbert, from_hilbert, *params)
    factor = 1.0 / math.sqrt(n_pt * n_case * LEN)
    result = pl.pallas_call(
        functools.partial(results_kernel, factor),
        out_shape=(
            rows,
            rows,
            shape((D, 3 * D), F32),
            shape((3 * D,), F32),
            shape((D, D), F32),
            shape((D,), F32),
            shape((D,), F32),
            shape((D,), F32),
        ),
        in_specs=[vmem] * 4,
        out_specs=(hbm, hbm, vmem, hbm, vmem, hbm, hbm, hbm),
        scratch_shapes=[pltpu.VMEM((4, 3 * D), F32), pltpu.SemaphoreType.DMA((6,))],
        compiler_params=pltpu.CompilerParams(vmem_limit_bytes=VMEM_LIMIT),
    )(output, grad_points, sums1, sums2)
    return (result[0][None], result[1][None], *result[2:])


def solution(mesh):
    n_pt, n_case = mesh.shape["pt"], mesh.shape["case"]
    members = n_pt // 2
    n_y = 8 if members >= 32 else 2
    rows = P("case", "pt", None)
    index = P("case", "pt")
    return jax.shard_map(
        functools.partial(on_device, n_pt, n_case, members // n_y, n_y),
        mesh=mesh,
        in_specs=(rows, rows, index, index) + (P(),) * 6,
        out_specs=(rows, rows) + (P(),) * 6,
        check_vma=False,
    )
```

time: 64 us -> 54.8 us (0.86)
  Pallas kernels: 63.2 us -> 54 us
    pallas_call x1, Pallas kernels: 60.2 us -> 51 us  [on_device(): pl.pallas_call(functools.partial(kernel, n_pt, n_case, n_x, n_y), out_sha...]
where the time goes in v2:
time: 54.8 us; the launch traced here: 54.6 us
  Pallas kernels  54 us (99%)
  between operations  0.64 us (1%)
    pallas_call x1, Pallas kernels, on_device(): pl.pallas_call(functools.partial(kernel, n_pt, n_case, n_x, n_y), out_sha...  51 us
    pallas_call x1, Pallas kernels, on_device(): pl.pallas_call(functools.partial(results_kernel, factor), out_shape=(rows...  3 us

profile of v2, /device:TPU:1, one launch (start us, length us, event | category | flops | bytes accessed | tf_op | source)
XLA Modules:
  0.0 54.6 jit_solution(14033988811655592639)
XLA Ops:
  0.6 51.0 %shard_map.161 = (bf16[512,256]{1,0:T(8,128)(2,1)}, bf16[512,256]{1,0:T(8,128)(2,1)}, bf16[2,32,16,128]{3,2,1,0:T(8,128)(2,1)}, bf16[2,33,16,128]{3,2,1,0:T(8,128)(2,1)}) custom-call(bf16[512,256]{1,0:T(8,128)(2,1)} %bitcast.4, bf16[512,256]{1,0:T(8,128)(2,1)} %bitcast.5, s32[1,512]{1,0:T(1,128)} %to_hilbert.1, s32[1,512]{1,0:T(1,128)} %from_hilbert.1, ...), custom_call_target="tpu_custom_call" | custom-call | tf_op jit(solution)/shard_map/pallas_call | solution.py:594
  51.6 3.0 %shard_map.162 = (bf16[512,256]{1,0:T(8,128)(2,1)}, bf16[512,256]{1,0:T(8,128)(2,1)}, f32[256,768]{1,0:T(8,128)}, f32[768]{0:T(1024)}, f32[256,256]{1,0:T(8,128)...) custom-call(bf16[512,256]{1,0:T(8,128)(2,1)} %get-tuple-element.20.output_in, bf16[512,256]{1,0:T(8,128)(2,1)} %get-tuple-element.21.grad_in, ...), custom_call_target="tpu_custom_call" | custom-call | tf_op jit(solution)/shard_map/pallas_call | solution.py:657

commit v3 on v2

--- a/solution.py
+++ b/solution.py
@@ -124,7 +124,6 @@
     pt = lax.axis_index("pt")
     case = lax.axis_index("case")
     core = lax.rem(pt, 2)
-    members = n_pt // 2
     member = lax.div(pt, 2)
     sibling = pt + 1 - 2 * core
     outer = lax.rem(pt + n_pt - 1 + 2 * core, n_pt)
@@ -140,8 +139,21 @@
         to = lax.rem(case + r, n_case)
         return to, {"pt": pt, "case": to}
 
-    m_peers = [m_peer(place) for place in ring_order(n_x, n_y)]
+    def xz_peer(place):
+        x_to = lax.rem(x_at + place[0], n_x)
+        z_to = lax.rem(case + place[1], n_case)
+        return x_to * n_case + z_to, {"pt": (x_to * n_y + y_at) * 2 + core, "case": z_to}
+
+    def y_peer(r):
+        to = lax.rem(y_at + r, n_y)
+        return to, {"pt": (x_at * n_y + to) * 2 + core, "case": case}
+
+    xy_peers = [m_peer(place) for place in ring_order(n_x, n_y)]
     z_peers = [z_peer(r) for _, r in ring_order(1, n_case)]
+    xz_peers = [xz_peer(place) for place in ring_order(n_x, n_case)]
+    y_peers = [y_peer(r) for _, r in ring_order(1, n_y)]
+    planes = ((member, xy_peers), (x_at * n_case + case, xz_peers))
+    lines = ((case, z_peers), (y_at, y_peers))
 
     def for_peers(peers, body):
         for peer in peers:
@@ -293,7 +305,8 @@
         attended = jnp.transpose(attended_t_s[i])
         branch = nn(attended, w_out[...]) + b_out_s[...]
         out_win[rows_of(halves[i], HALF), :] = (hilbert_p[i] + branch).astype(BF16)
-        ex_out[i] = to_side(i, out_win, HALF, out_win, 4)
+        if i == 0:
+            ex_out[i] = to_side(i, out_win, HALF, out_win, 4)
 
     def second_pass(i, block):
         b0 = block * 128
@@ -359,13 +372,14 @@
             - standard * jnp.mean(scaled * standard, axis=-1, keepdims=True)
         )
         grad_win[rows_of(halves[i], HALF), :] = (hilbert_c[i] + d_input).astype(BF16)
-        ex_grad[i] = to_side(i, grad_win, HALF, grad_win, 6)
+        if i == 0:
+            ex_grad[i] = to_side(i, grad_win, HALF, grad_win, 6)
 
     chunks = (
         (acc1, core_send1, core_recv1, m_send1, m_recv1, z_recv1, sums1),
         (acc2, core_send2, core_recv2, m_send2, m_recv2, z_recv2, sums2),
     )
-    per = TILES // members
+    pers = (TILES // (n_x * n_y), TILES // (n_x * n_case))
 
     def sem(chunk, stage):
         return ar_send.at[chunk * 5 + stage], ar_recv.at[chunk * 5 + stage]
@@ -394,68 +408,69 @@
 
     def m_start(chunk, copy):
         acc, _, recv0, send, recv = chunks[chunk][:5]
+        at, peers = planes[chunk]
         if chunk == 0:
             copy.wait()
         half = (acc[core] + recv0[pl.ds(0, TILES)].astype(F32)).astype(BF16)
-        send[...] = half.reshape(members, per, 16, 128)
-        recv[pl.ds(member, 1)] = send[pl.ds(member, 1)]
+        send[...] = half.reshape(len(peers) + 1, pers[chunk], 16, 128)
+        recv[pl.ds(at, 1)] = send[pl.ds(at, 1)]
         s, r = sem(chunk, 1)
-        for_peers(
-            m_peers,
-            lambda to, where: remote(send.at[to], recv.at[member], s, r, where).start(),
-        )
+        for to, where in peers:
+            remote(send.at[to], recv.at[at], s, r, where).start()
 
     def z_start(chunk):
         recv0, recv = chunks[chunk][4:6]
-        wait_total(recv0.at[pl.ds(0, members - 1)], sem(chunk, 1)[1])
-        recv[case] = jnp.sum(recv0[...].astype(F32), axis=0).astype(BF16)
+        at, peers = lines[chunk]
+        wait_total(recv0.at[pl.ds(0, len(planes[chunk][1]))], sem(chunk, 1)[1])
+        recv[at] = jnp.sum(recv0[...].astype(F32), axis=0).astype(BF16)
         s, r = sem(chunk, 2)
-        slot = recv.at[case]
-        for_peers(z_peers, lambda to, where: remote(slot, slot, s, r, where).start())
+        slot = recv.at[at]
+        for _, where in peers:
+            remote(slot, slot, s, r, where).start()
 
     def m_back(chunk):
         recv0, result = chunks[chunk][5:7]
-        wait_total(recv0.at[pl.ds(0, n_case - 1)], sem(chunk, 2)[1])
-        at = pl.ds(member * per, per)
-        result[core, at] = jnp.sum(recv0[...].astype(F32), axis=0).astype(BF16)
+        at, peers = planes[chunk]
+        wait_total(recv0.at[pl.ds(0, len(lines[chunk][1]))], sem(chunk, 2)[1])
+        rows = pl.ds(at * pers[chunk], pers[chunk])
+        result[core, rows] = jnp.sum(recv0[...].astype(F32), axis=0).astype(BF16)
         s, r = sem(chunk, 3)
-        slot = result.at[core, at]
-        for_peers(m_peers, lambda to, where: remote(slot, slot, s, r, where).start())
+        slot = result.at[core, rows]
+        for _, where in peers:
+            remote(slot, slot, s, r, where).start()
 
     def core_back(chunk):
         result = chunks[chunk][6]
-        wait_total(result.at[core, pl.ds(0, (members - 1) * per)], sem(chunk, 3)[1])
+        wait_total(result.at[core, pl.ds(0, len(planes[chunk][1]) * pers[chunk])], sem(chunk, 3)[1])
         slot = result.at[core, pl.ds(0, TILES)]
         copy = remote(slot, slot, *sem(chunk, 4), to_sib)
         copy.start()
         return copy
 
-    def vec_z_start(copy):
+    def vec_line_start(copy):
         copy.wait()
+        at, peers = lines[1]
         mine = pl.multiple_of(core * 8, 8)
-        vec_z[case] = high_low(vector_s[pl.ds(mine, 8), :] + joined(core_recv2[TILES]))
-        slot = vec_z.at[case]
-        for_peers(
-            z_peers,
-            lambda to, where: remote(slot, slot, ar_send.at[10], ar_recv.at[10], where).start(),
-        )
-
-    def vec_m_start():
-        wait_total(vec_z.at[pl.ds(0, n_case - 1)], ar_recv.at[10])
+        vec_z[at] = high_low(vector_s[pl.ds(mine, 8), :] + joined(core_recv2[TILES]))
+        slot = vec_z.at[at]
+        for _, where in peers:
+            remote(slot, slot, ar_send.at[10], ar_recv.at[10], where).start()
+
+    def vec_plane_start():
+        at, peers = planes[1]
+        count = len(lines[1][1])
+        wait_total(vec_z.at[pl.ds(0, count)], ar_recv.at[10])
         total = joined(vec_z[0])
-        for i in range(1, n_case):
+        for i in range(1, count + 1):
             total = total + joined(vec_z[i])
-        vec_m[member] = high_low(total)
-        slot = vec_m.at[member]
-        for_peers(
-            m_peers,
-            lambda to, where: remote(slot, slot, ar_send.at[11], ar_recv.at[11], where).start(),
-        )
+        vec_m[at] = high_low(total)
+        slot = vec_m.at[at]
+        for _, where in peers:
+            remote(slot, slot, ar_send.at[11], ar_recv.at[11], where).start()
 
     def vec_back():
-        wait_total(vec_m.at[pl.ds(0, members - 1)], ar_recv.at[11])
-        total = vec_m[...].astype(F32)
-        total = jnp.sum(total, axis=0)
+        wait_total(vec_m.at[pl.ds(0, len(planes[1][1]))], ar_recv.at[11])
+        total = jnp.sum(vec_m[...].astype(F32), axis=0)
         sums2[core, TILES] = high_low(total[:8] + total[8:])
         slot = sums2.at[core, TILES]
         copy = remote(slot, slot, ar_send.at[12], ar_recv.at[12], to_sib)
@@ -464,9 +479,10 @@
 
     def finish(chunk, copy):
         send1, _, recv2, result = chunks[chunk][3:7]
-        wait_total(send1.at[pl.ds(0, members - 1)], sem(chunk, 1)[0])
-        wait_total(recv2.at[pl.ds(0, n_case - 1)], sem(chunk, 2)[0])
-        wait_total(result.at[core, pl.ds(0, (members - 1) * per)], sem(chunk, 3)[0])
+        count = len(planes[chunk][1])
+        wait_total(send1.at[pl.ds(0, count)], sem(chunk, 1)[0])
+        wait_total(recv2.at[pl.ds(0, len(lines[chunk][1]))], sem(chunk, 2)[0])
+        wait_total(result.at[core, pl.ds(0, count * pers[chunk])], sem(chunk, 3)[0])
         copy.wait()
 
     project(0)
@@ -503,21 +519,23 @@
         store.start()
         return store
 
-    vec_z_start(core_copy2)
+    vec_line_start(core_copy2)
     m_start(1, None)
+    ex_out[1] = to_side(1, out_win, HALF, out_win, 4)
+    ex_grad[1] = to_side(1, grad_win, HALF, grad_win, 6)
     z_start(0)
+    vec_plane_start()
+    z_start(1)
     store_out = to_z_order(ex_out, out_win, out_stage, output, 10)
-    vec_m_start()
     m_back(0)
-    z_start(1)
+    m_back(1)
     store_grad = to_z_order(ex_grad, grad_win, grad_stage, grad_points, 11)
-    m_back(1)
     last1 = core_back(0)
     vec_last = vec_back()
     last2 = core_back(1)
     finish(0, last1)
-    wait_total(vec_z.at[pl.ds(0, n_case - 1)], ar_send.at[10])
-    wait_total(vec_m.at[pl.ds(0, members - 1)], ar_send.at[11])
+    wait_total(vec_z.at[pl.ds(0, len(lines[1][1]))], ar_send.at[10])
+    wait_total(vec_m.at[pl.ds(0, len(planes[1][1]))], ar_send.at[11])
     for pair in (ex_p, ex_c, ex_out, ex_grad):
         for copy in pair:
             copy.wait_send()
@@ -531,8 +549,8 @@
     factor,
     output_in,
     grad_in,
-    sums1,
-    sums2,
+    sums1_in,
+    sums2_in,
     output,
     grad_points,
     grad_w_qkv,
@@ -541,15 +559,41 @@
     grad_b_out,
     grad_gain,
     grad_bias,
+    output_s,
+    grad_s,
+    sums1,
+    sums2,
+    w_qkv_s,
+    w_out_s,
     vec_s,
-    sems,
+    in_sems,
+    out_sems,
 ):
-    copies = [
-        pltpu.make_async_copy(output_in, output, sems.at[0]),
-        pltpu.make_async_copy(grad_in, grad_points, sems.at[1]),
-    ]
-    for copy in copies:
-        copy.start()
+    loads = [(sums1_in, sums1), (sums2_in, sums2), (output_in, output_s), (grad_in, grad_s)]
+    loads = [pltpu.make_async_copy(a, b, in_sems.at[i]) for i, (a, b) in enumerate(loads)]
+    for load in loads:
+        load.start()
+    stores = []
+
+    def store(a, b):
+        stores.append(pltpu.make_async_copy(a, b, out_sems.at[len(stores)]))
+        stores[-1].start()
+
+    def block(sums, c, half):
+        return sums[c, pl.ds(half * 16, 16)].reshape(256, 128).astype(F32) * factor
+
+    def weight(sums, c, stage, first, result):
+        for half in range(2):
+            stage[:, pl.ds(first + half * 128, 128)] = block(sums, c, half)
+        columns = pl.ds(first, D)
+        store(stage.at[:, columns], result.at[:, columns])
+
+    loads[0].wait()
+    weight(sums1, 0, w_qkv_s, 512, grad_w_qkv)
+    weight(sums1, 1, w_out_s, 0, grad_w_out)
+    loads[1].wait()
+    weight(sums2, 0, w_qkv_s, 0, grad_w_qkv)
+    weight(sums2, 1, w_qkv_s, 256, grad_w_qkv)
     vectors = []
     for c in range(2):
         tile = sums2[c, TILES].astype(F32)
@@ -558,31 +602,21 @@
         vec_s[0:1, part * 128 : part * 128 + 128] = vectors[0][part : part + 1]
         row = 1 + part // 2
         vec_s[row : row + 1, (part % 2) * 128 : (part % 2) * 128 + 128] = vectors[1][part : part + 1]
-    small = [
-        pltpu.make_async_copy(vec_s.at[0], grad_b_qkv, sems.at[2]),
-        pltpu.make_async_copy(vec_s.at[1, pl.ds(0, D)], grad_b_out, sems.at[3]),
-        pltpu.make_async_copy(vec_s.at[2, pl.ds(0, D)], grad_gain, sems.at[4]),
-        pltpu.make_async_copy(vec_s.at[3, pl.ds(0, D)], grad_bias, sems.at[5]),
-    ]
-    for copy in small:
-        copy.start()
-
-    def block(sums, c, half):
-        return sums[c, pl.ds(half * 16, 16)].reshape(256, 128).astype(F32) * factor
-
-    for half in range(2):
-        lanes = half * 128
-        grad_w_qkv[:, pl.ds(lanes, 128)] = block(sums2, 0, half)
-        grad_w_qkv[:, pl.ds(256 + lanes, 128)] = block(sums2, 1, half)
-        grad_w_qkv[:, pl.ds(512 + lanes, 128)] = block(sums1, 0, half)
-        grad_w_out[:, pl.ds(lanes, 128)] = block(sums1, 1, half)
-    for copy in copies + small:
+    store(vec_s.at[0], grad_b_qkv)
+    store(vec_s.at[1, pl.ds(0, D)], grad_b_out)
+    store(vec_s.at[2, pl.ds(0, D)], grad_gain)
+    store(vec_s.at[3, pl.ds(0, D)], grad_bias)
+    loads[2].wait()
+    store(output_s, output)
+    loads[3].wait()
+    store(grad_s, grad_points)
+    for copy in stores:
         copy.wait()
 
 
 def on_device(n_pt, n_case, n_x, n_y, points, cotangent, to_hilbert, from_hilbert, *params):
-    members = n_pt // 2
-    per = TILES // members
+    plane1, plane2 = n_x * n_y, n_x * n_case
+    per1, per2 = TILES // plane1, TILES // plane2
     vmem = pl.BlockSpec(memory_space=pltpu.VMEM)
     hbm = pl.BlockSpec(memory_space=pl.ANY)
     shape = jax.ShapeDtypeStruct
@@ -632,14 +666,14 @@
             tiles(TILES + 1),
             tiles(TILES),
             tiles(TILES + 1),
-            tiles(members, per),
-            tiles(members, per),
-            tiles(members, per),
-            tiles(members, per),
-            tiles(n_case, per),
-            tiles(n_case, per),
-            tiles(n_case),
-            tiles(members),
+            tiles(plane1, per1),
+            tiles(plane2, per2),
+            tiles(plane1, per1),
+            tiles(plane2, per2),
+            tiles(n_case, per1),
+            tiles(n_y, per2),
+            tiles(n_y),
+            tiles(plane2),
             pltpu.VMEM((LEN, D), BF16),
             pltpu.VMEM((LEN, D), BF16),
             pltpu.SemaphoreType.DMA((12,)),
@@ -666,9 +700,19 @@
             shape((D,), F32),
             shape((D,), F32),
         ),
-        in_specs=[vmem] * 4,
-        out_specs=(hbm, hbm, vmem, hbm, vmem, hbm, hbm, hbm),
-        scratch_shapes=[pltpu.VMEM((4, 3 * D), F32), pltpu.SemaphoreType.DMA((6,))],
+        in_specs=[hbm] * 4,
+        out_specs=(hbm,) * 8,
+        scratch_shapes=[
+            pltpu.VMEM((LEN, D), BF16),
+            pltpu.VMEM((LEN, D), BF16),
+            tiles(2, TILES),
+            tiles(2, TILES + 1),
+            pltpu.VMEM((D, 3 * D), F32),
+            pltpu.VMEM((D, D), F32),
+            pltpu.VMEM((4, 3 * D), F32),
+            pltpu.SemaphoreType.DMA((4,)),
+            pltpu.SemaphoreType.DMA((10,)),
+        ],
         compiler_params=pltpu.CompilerParams(vmem_limit_bytes=VMEM_LIMIT),
     )(output, grad_points, sums1, sums2)
     return (result[0][None], result[1][None], *result[2:])

time: 54.8 us -> 51.7 us (0.943)
  Pallas kernels: 54 us -> 50.9 us
    pallas_call x1, Pallas kernels: 51 us -> 48.7 us  [on_device(): pl.pallas_call(functools.partial(kernel, n_pt, n_case, n_x, n_y), out_sha...]
    pallas_call x1, Pallas kernels: 3 us -> 2.24 us  [on_device(): pl.pallas_call(functools.partial(results_kernel, factor), out_shape=(rows...]
where the time goes in v3:
time: 51.7 us; the launch traced here: 51.6 us
  Pallas kernels  50.9 us (98%)
  between operations  0.64 us (1%)
    pallas_call x1, Pallas kernels, on_device(): pl.pallas_call(functools.partial(kernel, n_pt, n_case, n_x, n_y), out_sha...  48.7 us
    pallas_call x1, Pallas kernels, on_device(): pl.pallas_call(functools.partial(results_kernel, factor), out_shape=(rows...  2.24 us

profile of v3, /device:TPU:1, one launch (start us, length us, event | category | flops | bytes accessed | tf_op | source)
XLA Modules:
  0.0 51.6 jit_solution(15277738199729124795)
XLA Ops:
  0.6 48.7 %shard_map.161 = (bf16[512,256]{1,0:T(8,128)(2,1)}, bf16[512,256]{1,0:T(8,128)(2,1)}, bf16[2,32,16,128]{3,2,1,0:T(8,128)(2,1)}, bf16[2,33,16,128]{3,2,1,0:T(8,128)(2,1)}) custom-call(bf16[512,256]{1,0:T(8,128)(2,1)} %bitcast.4, bf16[512,256]{1,0:T(8,128)(2,1)} %bitcast.5, s32[1,512]{1,0:T(1,128)} %to_hilbert.1, s32[1,512]{1,0:T(1,128)} %from_hilbert.1, ...), custom_call_target="tpu_custom_call" | custom-call | tf_op jit(solution)/shard_map/pallas_call | solution.py:628
  49.3 2.2 %shard_map.162 = (bf16[512,256]{1,0:T(8,128)(2,1)}, bf16[512,256]{1,0:T(8,128)(2,1)}, f32[256,768]{1,0:T(8,128)}, f32[768]{0:T(1024)}, f32[256,256]{1,0:T(8,128)...) custom-call(bf16[512,256]{1,0:T(8,128)(2,1)} %get-tuple-element.20.output_in, bf16[512,256]{1,0:T(8,128)(2,1)} %get-tuple-element.21.grad_in, ...), custom_call_target="tpu_custom_call" | custom-call | tf_op jit(solution)/shard_map/pallas_call | solution.py:691

commit v4 on v3

--- a/solution.py
+++ b/solution.py
@@ -112,6 +112,8 @@
     z_recv2,
     vec_z,
     vec_m,
+    own_sum1,
+    own_sum2,
     out_stage,
     grad_stage,
     local_sem,
@@ -167,6 +169,9 @@
     to_sib = {"pt": sibling, "case": case}
     signal(None, {"pt": outer, "case": case})
     signal(None, to_sib)
+    near = [m_peer((0, 1)), m_peer((0, n_y - 1)), m_peer((1, 0)), m_peer((n_x - 1, 0))]
+    near += [z_peer(1), z_peer(n_case - 1)]
+    for_peers(near, signal)
     loads = [
         (points, point_win.at[pl.ds(HALF, LEN)]),
         (cotangent, cot_win.at[pl.ds(HALF, LEN)]),
@@ -182,9 +187,6 @@
     loads = [pltpu.make_async_copy(a, b, local_sem.at[i]) for i, (a, b) in enumerate(loads)]
     for load in loads:
         load.start()
-    near = [m_peer((0, 1)), m_peer((0, n_y - 1)), m_peer((1, 0)), m_peer((n_x - 1, 0))]
-    near += [z_peer(1), z_peer(n_case - 1)]
-    for_peers(near, signal)
     pl.semaphore_wait(barrier, 2 + len(near))
 
     def tell(step, peers):
@@ -275,6 +277,9 @@
         normed = (standard * gain + bias_s[...]).astype(BF16)
         normed_t_s[i] = jnp.transpose(normed)
         proj_s[i] = (nn(normed, w_qkv[...]) + b_qkv_s[...]).astype(BF16)
+
+    def project_cotangent(i):
+        p = halves[i]
         ex_c[i].wait_recv()
         cot = hilbert_c[i] + nn(hots[i], cot_win[side_rows(p), :])
         hilbert_c[i] = cot
@@ -286,20 +291,14 @@
             q = proj_s[i, :, pl.ds(b0, 128)]
             k = proj_s[i, :, pl.ds(256 + b0, 128)]
             v_t = jnp.transpose(proj_s[i, :, pl.ds(512 + b0, 128)])
-            da = d_att_s[i, :, pl.ds(b0, 128)]
-            d_v = None
             for h in range(4):
-                mask = masks[h]
-                exponent = jnp.exp2(nt(k * mask, q) * EXP2_SCALE)
+                exponent = jnp.exp2(nt(k * masks[h], q) * EXP2_SCALE)
                 total = jnp.sum(exponent, axis=0, keepdims=True)
                 prob = exponent * (1.0 / total)
                 prob_s[block * 4 + h] = prob
                 prob_low = prob.astype(BF16)
                 att_t = nn(v_t[h * HEAD : (h + 1) * HEAD], prob_low)
                 attended_t_s[i, pl.ds(b0 + h * HEAD, HEAD), :] = att_t.astype(BF16)
-                d_v_h = nn(prob_low, da * mask)
-                d_v = d_v_h if d_v is None else d_v + d_v_h
-            d_proj_s[i, :, pl.ds(512 + b0, 128)] = d_v.astype(BF16)
 
     def block_output(i):
         attended = jnp.transpose(attended_t_s[i])
@@ -316,9 +315,12 @@
         da = d_att_s[i, :, pl.ds(b0, 128)]
         d_q_t = []
         d_k = None
+        d_v = None
         for h in range(4):
             mask = masks[h]
             prob = prob_s[block * 4 + h]
+            d_v_h = nn(prob.astype(BF16), da * mask)
+            d_v = d_v_h if d_v is None else d_v + d_v_h
             d_prob = nt(v * mask, da)
             row_sum = jnp.sum(prob * d_prob, axis=0, keepdims=True)
             d_s = (prob * (d_prob - row_sum) * SCALE).astype(BF16)
@@ -328,6 +330,7 @@
         d_q = jnp.transpose(jnp.concatenate(d_q_t, axis=0))
         d_proj_s[i, :, pl.ds(b0, 128)] = d_q.astype(BF16)
         d_proj_s[i, :, pl.ds(256 + b0, 128)] = d_k.astype(BF16)
+        d_proj_s[i, :, pl.ds(512 + b0, 128)] = d_v.astype(BF16)
 
     def add(ref, index, value, i):
         ref[index] = value if i == 0 else ref[index] + value
@@ -376,8 +379,8 @@
             ex_grad[i] = to_side(i, grad_win, HALF, grad_win, 6)
 
     chunks = (
-        (acc1, core_send1, core_recv1, m_send1, m_recv1, z_recv1, sums1),
-        (acc2, core_send2, core_recv2, m_send2, m_recv2, z_recv2, sums2),
+        (acc1, core_send1, core_recv1, m_send1, m_recv1, z_recv1, own_sum1),
+        (acc2, core_send2, core_recv2, m_send2, m_recv2, z_recv2, own_sum2),
     )
     pers = (TILES // (n_x * n_y), TILES // (n_x * n_case))
 
@@ -409,8 +412,7 @@
     def m_start(chunk, copy):
         acc, _, recv0, send, recv = chunks[chunk][:5]
         at, peers = planes[chunk]
-        if chunk == 0:
-            copy.wait()
+        copy.wait()
         half = (acc[core] + recv0[pl.ds(0, TILES)].astype(F32)).astype(BF16)
         send[...] = half.reshape(len(peers) + 1, pers[chunk], 16, 128)
         recv[pl.ds(at, 1)] = send[pl.ds(at, 1)]
@@ -433,22 +435,23 @@
         at, peers = planes[chunk]
         wait_total(recv0.at[pl.ds(0, len(lines[chunk][1]))], sem(chunk, 2)[1])
         rows = pl.ds(at * pers[chunk], pers[chunk])
-        result[core, rows] = jnp.sum(recv0[...].astype(F32), axis=0).astype(BF16)
+        result[rows] = jnp.sum(recv0[...].astype(F32), axis=0).astype(BF16)
         s, r = sem(chunk, 3)
-        slot = result.at[core, rows]
+        slot = result.at[rows]
         for _, where in peers:
             remote(slot, slot, s, r, where).start()
 
     def core_back(chunk):
         result = chunks[chunk][6]
-        wait_total(result.at[core, pl.ds(0, len(planes[chunk][1]) * pers[chunk])], sem(chunk, 3)[1])
-        slot = result.at[core, pl.ds(0, TILES)]
-        copy = remote(slot, slot, *sem(chunk, 4), to_sib)
+        final = (sums1, sums2)[chunk].at[core]
+        wait_total(result.at[pl.ds(0, len(planes[chunk][1]) * pers[chunk])], sem(chunk, 3)[1])
+        copy = remote(result, final, *sem(chunk, 4), to_sib)
         copy.start()
-        return copy
-
-    def vec_line_start(copy):
-        copy.wait()
+        keep = pltpu.make_async_copy(result, final, local_sem.at[12 + chunk])
+        keep.start()
+        return copy, keep
+
+    def vec_line_start():
         at, peers = lines[1]
         mine = pl.multiple_of(core * 8, 8)
         vec_z[at] = high_low(vector_s[pl.ds(mine, 8), :] + joined(core_recv2[TILES]))
@@ -471,23 +474,21 @@
     def vec_back():
         wait_total(vec_m.at[pl.ds(0, len(planes[1][1]))], ar_recv.at[11])
         total = jnp.sum(vec_m[...].astype(F32), axis=0)
-        sums2[core, TILES] = high_low(total[:8] + total[8:])
-        slot = sums2.at[core, TILES]
-        copy = remote(slot, slot, ar_send.at[12], ar_recv.at[12], to_sib)
-        copy.start()
-        return copy
-
-    def finish(chunk, copy):
+        own_sum2[TILES] = high_low(total[:8] + total[8:])
+
+    def finish(chunk, copies):
         send1, _, recv2, result = chunks[chunk][3:7]
         count = len(planes[chunk][1])
         wait_total(send1.at[pl.ds(0, count)], sem(chunk, 1)[0])
         wait_total(recv2.at[pl.ds(0, len(lines[chunk][1]))], sem(chunk, 2)[0])
-        wait_total(result.at[core, pl.ds(0, count * pers[chunk])], sem(chunk, 3)[0])
-        copy.wait()
+        wait_total(result.at[pl.ds(0, count * pers[chunk])], sem(chunk, 3)[0])
+        for copy in copies:
+            copy.wait()
 
     project(0)
     first_pass(0)
     block_output(0)
+    project_cotangent(0)
     heard_rings()
     second_pass(0, 0)
     second_pass(0, 1)
@@ -495,16 +496,16 @@
     backward_terms(0)
     norm_backward(0)
     project(1)
-    heard(len(steps) - 1, steps[-1])
     first_pass(1)
+    block_output(1)
+    project_cotangent(1)
+    second_pass(1, 0)
+    second_pass(1, 1)
     forward_terms(1)
     core_copy1 = core_start(0)
-    block_output(1)
-    second_pass(1, 0)
-    m_start(0, core_copy1)
-    second_pass(1, 1)
     backward_terms(1)
     core_copy2 = core_start(1)
+    heard(len(steps) - 1, steps[-1])
     norm_backward(1)
 
     def to_z_order(pair, win, stage, result, at):
@@ -519,19 +520,20 @@
         store.start()
         return store
 
-    vec_line_start(core_copy2)
-    m_start(1, None)
+    m_start(0, core_copy1)
+    m_start(1, core_copy2)
+    vec_line_start()
     ex_out[1] = to_side(1, out_win, HALF, out_win, 4)
     ex_grad[1] = to_side(1, grad_win, HALF, grad_win, 6)
     z_start(0)
+    z_start(1)
     vec_plane_start()
-    z_start(1)
-    store_out = to_z_order(ex_out, out_win, out_stage, output, 10)
     m_back(0)
     m_back(1)
+    store_out = to_z_order(ex_out, out_win, out_stage, output, 10)
     store_grad = to_z_order(ex_grad, grad_win, grad_stage, grad_points, 11)
+    vec_back()
     last1 = core_back(0)
-    vec_last = vec_back()
     last2 = core_back(1)
     finish(0, last1)
     wait_total(vec_z.at[pl.ds(0, len(lines[1][1]))], ar_send.at[10])
@@ -541,7 +543,6 @@
             copy.wait_send()
     store_out.wait()
     store_grad.wait()
-    vec_last.wait()
     finish(1, last2)
 
 
@@ -617,7 +618,6 @@
 def on_device(n_pt, n_case, n_x, n_y, points, cotangent, to_hilbert, from_hilbert, *params):
     plane1, plane2 = n_x * n_y, n_x * n_case
     per1, per2 = TILES // plane1, TILES // plane2
-    vmem = pl.BlockSpec(memory_space=pltpu.VMEM)
     hbm = pl.BlockSpec(memory_space=pl.ANY)
     shape = jax.ShapeDtypeStruct
     rows = shape((LEN, D), BF16)
@@ -634,7 +634,7 @@
             shape((2, TILES + 1, 16, 128), BF16),
         ),
         in_specs=[hbm] * 10,
-        out_specs=(hbm, hbm, vmem, vmem),
+        out_specs=(hbm,) * 4,
         scratch_shapes=[
             pltpu.VMEM((1, LEN), jnp.int32),
             pltpu.VMEM((1, LEN), jnp.int32),
@@ -674,9 +674,11 @@
             tiles(n_y, per2),
             tiles(n_y),
             tiles(plane2),
+            tiles(TILES),
+            tiles(TILES + 1),
             pltpu.VMEM((LEN, D), BF16),
             pltpu.VMEM((LEN, D), BF16),
-            pltpu.SemaphoreType.DMA((12,)),
+            pltpu.SemaphoreType.DMA((14,)),
             pltpu.SemaphoreType.DMA((8,)),
             pltpu.SemaphoreType.DMA((8,)),
             pltpu.SemaphoreType.DMA((14,)),

time: 51.7 us -> 51.3 us (level)
  no operation moved by 1% of the time
where the time goes in v4:
time: 51.3 us; the launch traced here: 51.2 us
  Pallas kernels  50.5 us (98%)
  between operations  0.64 us (1%)
    pallas_call x1, Pallas kernels, on_device(): pl.pallas_call(functools.partial(kernel, n_pt, n_case, n_x, n_y), out_sha...  48.3 us
    pallas_call x1, Pallas kernels, on_device(): pl.pallas_call(functools.partial(results_kernel, factor), out_shape=(rows...  2.24 us

profile of v4, /device:TPU:1, one launch (start us, length us, event | category | flops | bytes accessed | tf_op | source)
XLA Modules:
  0.0 51.2 jit_solution(15734110096061445135)
XLA Ops:
  0.6 48.3 %shard_map.161 = (bf16[512,256]{1,0:T(8,128)(2,1)}, bf16[512,256]{1,0:T(8,128)(2,1)}, bf16[2,32,16,128]{3,2,1,0:T(8,128)(2,1)}, bf16[2,33,16,128]{3,2,1,0:T(8,128)(2,1)}) custom-call(bf16[512,256]{1,0:T(8,128)(2,1)} %bitcast.4, bf16[512,256]{1,0:T(8,128)(2,1)} %bitcast.5, s32[1,512]{1,0:T(1,128)} %to_hilbert.1, s32[1,512]{1,0:T(1,128)} %from_hilbert.1, ...), custom_call_target="tpu_custom_call" | custom-call | tf_op jit(solution)/shard_map/pallas_call | solution.py:628
  48.9 2.2 %shard_map.162 = (bf16[512,256]{1,0:T(8,128)(2,1)}, bf16[512,256]{1,0:T(8,128)(2,1)}, f32[256,768]{1,0:T(8,128)}, f32[768]{0:T(1024)}, f32[256,256]{1,0:T(8,128)...) custom-call(bf16[512,256]{1,0:T(8,128)(2,1)} %get-tuple-element.20.output_in, bf16[512,256]{1,0:T(8,128)(2,1)} %get-tuple-element.21.grad_in, ...), custom_call_target="tpu_custom_call" | custom-call | tf_op jit(solution)/shard_map/pallas_call | solution.py:693

commit v5 on v4

--- a/solution.py
+++ b/solution.py
@@ -286,19 +286,24 @@
         d_att_s[i] = nt(cot.astype(BF16), w_out[...]).astype(BF16)
 
     def first_pass(i):
-        for block in range(2):
-            b0 = block * 128
-            q = proj_s[i, :, pl.ds(b0, 128)]
+        def scores(unit):
+            b0 = unit // 4 * 128
             k = proj_s[i, :, pl.ds(256 + b0, 128)]
-            v_t = jnp.transpose(proj_s[i, :, pl.ds(512 + b0, 128)])
-            for h in range(4):
-                exponent = jnp.exp2(nt(k * masks[h], q) * EXP2_SCALE)
-                total = jnp.sum(exponent, axis=0, keepdims=True)
-                prob = exponent * (1.0 / total)
-                prob_s[block * 4 + h] = prob
-                prob_low = prob.astype(BF16)
-                att_t = nn(v_t[h * HEAD : (h + 1) * HEAD], prob_low)
-                attended_t_s[i, pl.ds(b0 + h * HEAD, HEAD), :] = att_t.astype(BF16)
+            return nt(k * masks[unit % 4], proj_s[i, :, pl.ds(b0, 128)])
+
+        ahead = [scores(unit) for unit in range(4)]
+        for unit in range(HEADS):
+            if unit + 4 < HEADS:
+                ahead.append(scores(unit + 4))
+            if unit % 4 == 0:
+                v_t = jnp.transpose(proj_s[i, :, pl.ds(512 + unit // 4 * 128, 128)])
+            h = unit % 4
+            exponent = jnp.exp2(ahead[unit] * EXP2_SCALE)
+            total = jnp.sum(exponent, axis=0, keepdims=True)
+            prob = exponent * (1.0 / total)
+            prob_s[unit] = prob
+            att_t = nn(v_t[h * HEAD : (h + 1) * HEAD], prob.astype(BF16))
+            attended_t_s[i, pl.ds(unit * HEAD, HEAD), :] = att_t.astype(BF16)
 
     def block_output(i):
         attended = jnp.transpose(attended_t_s[i])
@@ -307,30 +312,40 @@
         if i == 0:
             ex_out[i] = to_side(i, out_win, HALF, out_win, 4)
 
-    def second_pass(i, block):
-        b0 = block * 128
-        q = proj_s[i, :, pl.ds(b0, 128)]
-        k_t = jnp.transpose(proj_s[i, :, pl.ds(256 + b0, 128)])
-        v = proj_s[i, :, pl.ds(512 + b0, 128)]
-        da = d_att_s[i, :, pl.ds(b0, 128)]
-        d_q_t = []
-        d_k = None
-        d_v = None
-        for h in range(4):
-            mask = masks[h]
-            prob = prob_s[block * 4 + h]
-            d_v_h = nn(prob.astype(BF16), da * mask)
-            d_v = d_v_h if d_v is None else d_v + d_v_h
-            d_prob = nt(v * mask, da)
+    def second_pass(i):
+        def d_probs(unit):
+            b0 = unit // 4 * 128
+            v = proj_s[i, :, pl.ds(512 + b0, 128)]
+            return nt(v * masks[unit % 4], d_att_s[i, :, pl.ds(b0, 128)])
+
+        def d_scores(unit):
+            prob, d_prob = prob_s[unit], ahead[unit]
             row_sum = jnp.sum(prob * d_prob, axis=0, keepdims=True)
-            d_s = (prob * (d_prob - row_sum) * SCALE).astype(BF16)
-            d_k_h = nn(d_s, q * mask)
-            d_k = d_k_h if d_k is None else d_k + d_k_h
-            d_q_t.append(nn(k_t[h * HEAD : (h + 1) * HEAD], d_s))
-        d_q = jnp.transpose(jnp.concatenate(d_q_t, axis=0))
-        d_proj_s[i, :, pl.ds(b0, 128)] = d_q.astype(BF16)
-        d_proj_s[i, :, pl.ds(256 + b0, 128)] = d_k.astype(BF16)
-        d_proj_s[i, :, pl.ds(512 + b0, 128)] = d_v.astype(BF16)
+            return (prob * (d_prob - row_sum) * SCALE).astype(BF16)
+
+        ahead = [d_probs(unit) for unit in range(4)]
+        low = [d_scores(0)]
+        for unit in range(HEADS):
+            h, b0 = unit % 4, unit // 4 * 128
+            if unit + 4 < HEADS:
+                ahead.append(d_probs(unit + 4))
+            if unit + 1 < HEADS:
+                low.append(d_scores(unit + 1))
+            if h == 0:
+                q = proj_s[i, :, pl.ds(b0, 128)]
+                k_t = jnp.transpose(proj_s[i, :, pl.ds(256 + b0, 128)])
+                da = d_att_s[i, :, pl.ds(b0, 128)]
+                d_q_t = []
+            d_v_h = nn(prob_s[unit].astype(BF16), da * masks[h])
+            d_k_h = nn(low[unit], q * masks[h])
+            d_v = d_v_h if h == 0 else d_v + d_v_h
+            d_k = d_k_h if h == 0 else d_k + d_k_h
+            d_q_t.append(nn(k_t[h * HEAD : (h + 1) * HEAD], low[unit]))
+            if h == 3:
+                d_q = jnp.transpose(jnp.concatenate(d_q_t, axis=0))
+                d_proj_s[i, :, pl.ds(b0, 128)] = d_q.astype(BF16)
+                d_proj_s[i, :, pl.ds(256 + b0, 128)] = d_k.astype(BF16)
+                d_proj_s[i, :, pl.ds(512 + b0, 128)] = d_v.astype(BF16)
 
     def add(ref, index, value, i):
         ref[index] = value if i == 0 else ref[index] + value
@@ -490,8 +505,7 @@
     block_output(0)
     project_cotangent(0)
     heard_rings()
-    second_pass(0, 0)
-    second_pass(0, 1)
+    second_pass(0)
     forward_terms(0)
     backward_terms(0)
     norm_backward(0)
@@ -499,8 +513,7 @@
     first_pass(1)
     block_output(1)
     project_cotangent(1)
-    second_pass(1, 0)
-    second_pass(1, 1)
+    second_pass(1)
     forward_terms(1)
     core_copy1 = core_start(0)
     backward_terms(1)

time: 51.3 us -> 47.6 us (0.928)
  Pallas kernels: 50.5 us -> 46.9 us
    pallas_call x1, Pallas kernels: 48.3 us -> 44.6 us  [on_device(): pl.pallas_call(functools.partial(kernel, n_pt, n_case, n_x, n_y), out_sha...]
where the time goes in v5:
time: 47.6 us; the launch traced here: 47.5 us
  Pallas kernels  46.9 us (99%)
  between operations  0.64 us (1%)
    pallas_call x1, Pallas kernels, on_device(): pl.pallas_call(functools.partial(kernel, n_pt, n_case, n_x, n_y), out_sha...  44.6 us
    pallas_call x1, Pallas kernels, on_device(): pl.pallas_call(functools.partial(results_kernel, factor), out_shape=(rows...  2.24 us

profile of v5, /device:TPU:1, one launch (start us, length us, event | category | flops | bytes accessed | tf_op | source)
XLA Modules:
  0.0 47.5 jit_solution(6066514104803166142)
XLA Ops:
  0.6 44.6 %shard_map.161 = (bf16[512,256]{1,0:T(8,128)(2,1)}, bf16[512,256]{1,0:T(8,128)(2,1)}, bf16[2,32,16,128]{3,2,1,0:T(8,128)(2,1)}, bf16[2,33,16,128]{3,2,1,0:T(8,128)(2,1)}) custom-call(bf16[512,256]{1,0:T(8,128)(2,1)} %bitcast.4, bf16[512,256]{1,0:T(8,128)(2,1)} %bitcast.5, s32[1,512]{1,0:T(1,128)} %to_hilbert.1, s32[1,512]{1,0:T(1,128)} %from_hilbert.1, ...), custom_call_target="tpu_custom_call" | custom-call | tf_op jit(solution)/shard_map/pallas_call | solution.py:641
  45.3 2.2 %shard_map.162 = (bf16[512,256]{1,0:T(8,128)(2,1)}, bf16[512,256]{1,0:T(8,128)(2,1)}, f32[256,768]{1,0:T(8,128)}, f32[768]{0:T(1024)}, f32[256,256]{1,0:T(8,128)...) custom-call(bf16[512,256]{1,0:T(8,128)(2,1)} %get-tuple-element.20.output_in, bf16[512,256]{1,0:T(8,128)(2,1)} %get-tuple-element.21.grad_in, ...), custom_call_target="tpu_custom_call" | custom-call | tf_op jit(solution)/shard_map/pallas_call | solution.py:706

commit v6 on v5

--- a/solution.py
+++ b/solution.py
@@ -291,10 +291,10 @@
             k = proj_s[i, :, pl.ds(256 + b0, 128)]
             return nt(k * masks[unit % 4], proj_s[i, :, pl.ds(b0, 128)])
 
-        ahead = [scores(unit) for unit in range(4)]
+        ahead = [scores(unit) for unit in range(6)]
         for unit in range(HEADS):
-            if unit + 4 < HEADS:
-                ahead.append(scores(unit + 4))
+            if unit + 6 < HEADS:
+                ahead.append(scores(unit + 6))
             if unit % 4 == 0:
                 v_t = jnp.transpose(proj_s[i, :, pl.ds(512 + unit // 4 * 128, 128)])
             h = unit % 4
@@ -323,12 +323,12 @@
             row_sum = jnp.sum(prob * d_prob, axis=0, keepdims=True)
             return (prob * (d_prob - row_sum) * SCALE).astype(BF16)
 
-        ahead = [d_probs(unit) for unit in range(4)]
+        ahead = [d_probs(unit) for unit in range(6)]
         low = [d_scores(0)]
         for unit in range(HEADS):
             h, b0 = unit % 4, unit // 4 * 128
-            if unit + 4 < HEADS:
-                ahead.append(d_probs(unit + 4))
+            if unit + 6 < HEADS:
+                ahead.append(d_probs(unit + 6))
             if unit + 1 < HEADS:
                 low.append(d_scores(unit + 1))
             if h == 0:
@@ -511,7 +511,6 @@
     norm_backward(0)
     project(1)
     first_pass(1)
-    block_output(1)
     project_cotangent(1)
     second_pass(1)
     forward_terms(1)
@@ -519,6 +518,7 @@
     backward_terms(1)
     core_copy2 = core_start(1)
     heard(len(steps) - 1, steps[-1])
+    block_output(1)
     norm_backward(1)
 
     def to_z_order(pair, win, stage, result, at):

time: 47.6 us -> 47.4 us (level)
  no operation moved by 1% of the time
where the time goes in v6:
time: 47.4 us; the launch traced here: 47.3 us
  Pallas kernels  46.6 us (98%)
  between operations  0.64 us (1%)
    pallas_call x1, Pallas kernels, on_device(): pl.pallas_call(functools.partial(kernel, n_pt, n_case, n_x, n_y), out_sha...  44.4 us
    pallas_call x1, Pallas kernels, on_device(): pl.pallas_call(functools.partial(results_kernel, factor), out_shape=(rows...  2.24 us

profile of v6, /device:TPU:1, one launch (start us, length us, event | category | flops | bytes accessed | tf_op | source)
XLA Modules:
  0.0 47.3 jit_solution(18002276118853853330)
XLA Ops:
  0.6 44.4 %shard_map.161 = (bf16[512,256]{1,0:T(8,128)(2,1)}, bf16[512,256]{1,0:T(8,128)(2,1)}, bf16[2,32,16,128]{3,2,1,0:T(8,128)(2,1)}, bf16[2,33,16,128]{3,2,1,0:T(8,128)(2,1)}) custom-call(bf16[512,256]{1,0:T(8,128)(2,1)} %bitcast.4, bf16[512,256]{1,0:T(8,128)(2,1)} %bitcast.5, s32[1,512]{1,0:T(1,128)} %to_hilbert.1, s32[1,512]{1,0:T(1,128)} %from_hilbert.1, ...), custom_call_target="tpu_custom_call" | custom-call | tf_op jit(solution)/shard_map/pallas_call | solution.py:641
  45.0 2.2 %shard_map.162 = (bf16[512,256]{1,0:T(8,128)(2,1)}, bf16[512,256]{1,0:T(8,128)(2,1)}, f32[256,768]{1,0:T(8,128)}, f32[768]{0:T(1024)}, f32[256,256]{1,0:T(8,128)...) custom-call(bf16[512,256]{1,0:T(8,128)(2,1)} %get-tuple-element.20.output_in, bf16[512,256]{1,0:T(8,128)(2,1)} %get-tuple-element.21.grad_in, ...), custom_call_target="tpu_custom_call" | custom-call | tf_op jit(solution)/shard_map/pallas_call | solution.py:706
